TPU v7x, 512 devices: a whole 4x4x16 slice. The times are simulated.
512 devices in a mesh: tok: 64 (over z, x), proto: 8 (over y, core).
Axes of the slice: x: 4, y: 4, z: 16, core: 2. Of those that a mesh axis runs over, the one named last changes fastest.
Arguments:
- student_feats: bfloat16 [64, 1568, 256], P('tok'), may hold values from -14 to 14
- teacher_feats: bfloat16 [64, 1568, 256], P('tok'), may hold values from -21 to 21
- token_mask: int32 [64, 1568], P('tok'), may hold values from 0 to 1, as said below
- dest_perm: int32 [64], replicated, may hold values from 0 to 63, each once
- clip_cot: float32 [64], P('tok'), may hold values from 4096 to 32768
- prototypes: bfloat16 [256, 32768], P(None, 'proto'), may hold values from -4 to 4
- center: float32 [32768], P('proto'), may hold values from -0.12 to 0.12
Outputs:
- feat_grads: bfloat16 [64, 1568, 256], P('tok')
- proto_grads: float32 [256, 32768], P('tok', 'proto')
- row_loss: float32 [32768], P('tok')
Inputs may be any that keep to these rules, and one draw needn't show every extreme that they name: `token_mask`: each clip masks between 64 and 960 of its 1568 tokens, some clip exactly 960, and 32768 tokens are masked in all.
All inputs are finite; a program needn't handle non-finite values.
Results may differ from a plain program's by a relative error of at most 0.0086.
Values may be sent and summed in bfloat16 or wider, within the bound.
A program may use at most 64 MiB of HBM per device.

v0:
```python
import jax
import jax.numpy as jnp
from jax import lax
from jax.sharding import PartitionSpec as P

RECV = 512


student_temp = 0.1
teacher_temp = 0.07


def unit_rows(values):
    length = jnp.sqrt(jnp.sum(values * values, axis=-1, keepdims=True) + 1e-06)
    return (values / length, length)


def on_device(student_feats, teacher_feats, token_mask, dest_perm, clip_cot, prototypes, center):
    devices = lax.axis_size("tok")
    my_index = lax.axis_index("tok")
    width = student_feats.shape[2]
    capacity = (2 * RECV - devices) // devices
    slot_total = devices * capacity
    token_flags = token_mask[0]
    own_count = jnp.sum(token_flags).astype(jnp.float32)
    summary = jnp.stack([own_count, clip_cot[0]])[None, :]
    clip_table = lax.all_gather(summary, "tok", axis=0, tiled=True)
    counts_int = clip_table[:, 0].astype(jnp.int32)
    row_weight = clip_table[:, 1] / clip_table[:, 0]
    offsets = jnp.cumsum(counts_int) - counts_int
    positions = jnp.arange(devices, dtype=jnp.int32)
    own_offset = jnp.sum(jnp.where(positions == my_index, offsets, 0))
    masked_rank = jnp.cumsum(token_flags) - 1
    cycle_pos = (own_offset + masked_rank) % devices
    target = jnp.sum(
        jnp.where(cycle_pos[:, None] == positions[None, :], dest_perm[None, :], 0), axis=1
    )
    send_place = jnp.where(token_flags > 0, target * capacity + masked_rank // devices, slot_total)

    def pack_rows(source):
        buffer = (
            jnp.zeros((slot_total, source.shape[1]), source.dtype)
            .at[send_place]
            .set(source, mode="drop")
        )
        return buffer.reshape(devices, capacity, source.shape[1])

    student_tokens = student_feats[0]
    teacher_tokens = teacher_feats[0]
    arrived_student, arrived_teacher = (
        lax.all_to_all(pack_rows(student_tokens), "tok", split_axis=0, concat_axis=0, tiled=True),
        lax.all_to_all(pack_rows(teacher_tokens), "tok", split_axis=0, concat_axis=0, tiled=True),
    )
    own_slot = jnp.sum(jnp.where(dest_perm == my_index, positions, 0))
    slot_index = jnp.arange(capacity, dtype=jnp.int32)
    local_rank = slot_index[None, :] * devices + (own_slot - offsets)[:, None] % devices
    live_slot = (local_rank < counts_int[:, None]).reshape(slot_total)
    dest_row = jnp.where(
        live_slot, ((offsets[:, None] + local_rank) // devices).reshape(slot_total), RECV
    )
    student_slab = (
        jnp.zeros((RECV, width), jnp.bfloat16)
        .at[dest_row]
        .set(arrived_student.reshape(slot_total, width), mode="drop")
    )
    teacher_slab = (
        jnp.zeros((RECV, width), jnp.bfloat16)
        .at[dest_row]
        .set(arrived_teacher.reshape(slot_total, width), mode="drop")
    )
    slot_weight = jnp.broadcast_to(row_weight[:, None], (devices, capacity)).reshape(slot_total)
    slab_weight = jnp.zeros((RECV,), jnp.float32).at[dest_row].set(slot_weight, mode="drop")
    unit_student, student_norm = unit_rows(student_slab.astype(jnp.float32))
    student_half = unit_student.astype(jnp.bfloat16)
    teacher_half = unit_rows(teacher_slab.astype(jnp.float32))[0].astype(jnp.bfloat16)
    scores = jnp.dot(student_half, prototypes, preferred_element_type=jnp.float32) / student_temp
    targets = (
        jnp.dot(teacher_half, prototypes, preferred_element_type=jnp.float32) - center[None, :]
    ) / teacher_temp
    peak_student, peak_teacher = lax.pmax(
        (jnp.max(scores, axis=1), jnp.max(targets, axis=1)), "proto"
    )
    local_tilted = jnp.exp(targets - peak_teacher[:, None])
    total_student, total_teacher, cross_sum = lax.psum(
        (
            jnp.sum(jnp.exp(scores - peak_student[:, None]), axis=1),
            jnp.sum(local_tilted, axis=1),
            jnp.sum(local_tilted * scores, axis=1),
        ),
        "proto",
    )
    row_loss = peak_student + jnp.log(total_student) - cross_sum / total_teacher
    student_prob = jnp.exp(scores - peak_student[:, None]) / total_student[:, None]
    teacher_prob = jnp.exp(targets - peak_teacher[:, None]) / total_teacher[:, None]
    grad_half = (slab_weight[:, None] * (student_prob - teacher_prob) / student_temp).astype(
        jnp.bfloat16
    )
    proto_part = lax.dot_general(
        grad_half, prototypes, (((1,), (1,)), ((), ())), preferred_element_type=jnp.float32
    )
    unit_grad = lax.psum(proto_part, "proto")
    feat_grad = (
        (unit_grad - unit_student * jnp.sum(unit_student * unit_grad, axis=1, keepdims=True))
        / student_norm
    ).astype(jnp.bfloat16)
    proto_grads = lax.psum_scatter(
        lax.dot_general(
            student_half, grad_half, (((0,), (0,)), ((), ())), preferred_element_type=jnp.float32
        ),
        "tok",
        scatter_dimension=0,
        tiled=True,
    )
    gathered_rows = feat_grad[jnp.minimum(dest_row, RECV - 1)]
    back_rows = jnp.where(live_slot[:, None], gathered_rows, jnp.zeros((), jnp.bfloat16)).reshape(
        devices, capacity, width
    )
    returned = lax.all_to_all(back_rows, "tok", split_axis=0, concat_axis=0, tiled=True)
    flat_back = returned.reshape(slot_total, width)
    picked_rows = flat_back[jnp.minimum(send_place, slot_total - 1)]
    token_grad = jnp.where(token_flags[:, None] > 0, picked_rows, jnp.zeros((), jnp.bfloat16))
    return (token_grad[None], proto_grads, row_loss)


def solution(mesh):
    in_specs = (
        P("tok", None, None),
        P("tok", None, None),
        P("tok", None),
        P(),
        P("tok"),
        P(None, "proto"),
        P("proto"),
    )
    out_specs = (P("tok", None, None), P("tok", "proto"), P("tok"))
    return jax.shard_map(
        on_device, mesh=mesh, in_specs=in_specs, out_specs=out_specs, check_vma=False
    )
```

profile of v0, /device:TPU:16, one launch (start us, length us, event | category | flops | bytes accessed | tf_op | source)
XLA Modules:
  0.0 695.6 jit_solution(5566385387518978526)
XLA Ops:
  8.0 1.3 fusion.37
  10.0 1.4 fusion.40
  12.0 0.2 maximum_dynamic-update-slice_fusion
  12.2 149.6 %all-reduce.1 = f32[128]{0:T(128)S(1)} all-reduce(f32[128]{0:T(128)S(1)} %maximum_dynamic-update-slice_fusion), channel_id=2, replica_groups=mesh['tok'=64,'proto'=8] {'tok'}, use_global_device_ids=true, to_apply=%add.1 | all-reduce | flops 128 | bytes 1024
  161.8 0.3 reduce-window.14
  162.1 0.1 slice.28
  162.2 0.1 slice_reduce_fusion
  162.3 0.1 add_bitcast_fusion
  162.4 0.1 reshape.329
  162.5 0.2 fusion.25
  162.7 0.1 reduce-window.11
  162.8 1.3 fusion.34
  164.1 0.8 subtract_reduce_fusion
  164.9 0.6 fusion.35
  165.5 0.7 add_select_fusion.2
  166.2 0.8 select_reduce_fusion
  167.0 10.6 %scatter_custom_fusion.1 = bf16[960,256]{1,0:T(8,128)(2,1)S(1)} fusion(s32[1568]{0:T(1024)S(1)} %compare_select_fusion.3, bf16[1,1568,256]{2,1,0:T(8,128)(2,1)} %param.7, bf16[]{:T(256)} %constant.85.clone.1), kind=kCustom, calls=%fused_computation.19 | custom fusion | bytes 1294338 | tf_op jit(solution)/shard_map/scatter | solution.py:44
  177.7 1.0 reshape.268
  178.6 6.7 all-to-all-start
  185.4 10.6 %scatter_custom_fusion.3 = bf16[960,256]{1,0:T(8,128)(2,1)S(1)} fusion(s32[1568]{0:T(1024)S(1)} %compare_select_fusion.3, bf16[1,1568,256]{2,1,0:T(8,128)(2,1)} %param.8, bf16[]{:T(256)} %constant.85.clone.1), kind=kCustom, calls=%fused_computation.17 | custom fusion | bytes 1294338 | tf_op jit(solution)/shard_map/scatter | solution.py:44
  196.0 0.9 reshape.270
  197.0 21.0 %all-to-all-done = bf16[64,15,256]{2,1,0:T(8,128)(2,1)S(1)} async-done(((bf16[64,15,256]{2,1,0:T(8,128)(2,1)}), bf16[64,15,256]{2,1,0:T(8,128)(2,1)S(1)}, u32[]{:S(2)}, u32[]{:S(2)}) %all-to-all-start) | async-done | bytes 491552 | tf_op jit(solution)/shard_map/all_to_all | solution.py:51
  218.0 5.8 all-to-all-start.1
  223.9 0.0 all-reduce.8.cloned.1.call-start
  223.9 0.1 broadcast_in_dim.98
  224.0 0.1 reshape.293
  224.1 0.1 add_compare_fusion
  224.2 0.1 lt.73
  224.4 0.1 add_add_fusion
  224.5 0.1 add.165
  224.7 5.4 scatter_custom_fusion
  230.1 0.9 reshape.309
  231.0 5.8 scatter_custom_fusion.2
  236.9 0.1 fusion.7
  237.0 9.8 %all-to-all-done.1 = bf16[64,15,256]{2,1,0:T(8,128)(2,1)S(1)} async-done(((bf16[64,15,256]{2,1,0:T(8,128)(2,1)}), bf16[64,15,256]{2,1,0:T(8,128)(2,1)S(1)}, u32[]{:S(2)}, u32[]{:S(2)}) %all-to-all-start.1) | async-done | bytes 491552 | tf_op jit(solution)/shard_map/all_to_all | solution.py:52
  246.9 0.9 reshape.325
  247.8 5.8 scatter_custom_fusion.4
  253.6 0.1 fusion.8
  253.8 4.5 multiply_reduce_fusion.1
  258.3 4.6 fusion.1
  262.9 10.1 %all-reduce.4 = (f32[512]{0:T(512)S(1)}, f32[512]{0:T(512)S(1)}) all-reduce(f32[512]{0:T(512)S(1)} %get-tuple-element.25, f32[512]{0:T(512)S(1)} %get-tuple-element.27), channel_id=1, replica_groups=mesh['tok'=64,'proto'=8] {'proto'}, use_global_device_ids=true, to_apply=%region_19.20 | all-reduce | flops 1024 | bytes 8192 | tf_op jit(solution)/shard_map/pmax | solution.py:80
  273.1 8.6 %multiply_reduce_fusion = (f32[512]{0:T(512)S(1)}, f32[512]{0:T(512)S(1)}, f32[512]{0:T(512)S(1)}) fusion(f32[512,4096]{1,0:T(8,128)} %get-tuple-element.28, f32[512,4096]{1,0:T(8,128)} %get-tuple-element.26, f32[512]{0:T(512)S(1)} %get-tuple-element.14, f32[4096]{0:T(1024)S(1)} %copy-done.2, f32[512]{0:T(512)S(1)} %get-tuple-element.15), kind=kLoop, calls=%fused_computation.7 | loop fusion | flops 18872832 | bytes 16803840 | tf_op jit(solution)/shard_map/reduce_sum | solution.py:88
  281.7 10.9 %all-reduce.3 = (f32[512]{0:T(512)S(1)}, f32[512]{0:T(512)S(1)}, f32[512]{0:T(512)S(1)}) all-reduce(f32[512]{0:T(512)S(1)} %get-tuple-element.4, f32[512]{0:T(512)S(1)} %get-tuple-element.5, f32[512]{0:T(512)S(1)} %get-tuple-element.3), channel_id=1, replica_groups=mesh['tok'=64,'proto'=8] {'proto'}, use_global_device_ids=true, to_apply=%region_21.22 | all-reduce | flops 1536 | bytes 12288 | tf_op jit(solution)/shard_map/psum | solution.py:84
  292.7 8.9 %multiply_convert_fusion = bf16[512,4096]{1,0:T(8,128)(2,1)S(1)} fusion(f32[512,4096]{1,0:T(8,128)} %get-tuple-element.28, f32[512,4096]{1,0:T(8,128)} %get-tuple-element.26, f32[512]{0:T(512)S(1)} %get-tuple-element.11, f32[512]{0:T(512)S(1)} %get-tuple-element.14, f32[4096]{0:T(1024)S(1)} %copy-done.2, f32[512]{0:T(512)S(1)} %get-tuple-element.12, ...), kind=kLoop, calls=%fused_computation.8 | loop fusion | flops 23068672 | bytes 20998144 | tf_op jit(solution)/shard_map/convert_element_type | solution.py:95
  301.6 2.0 copy-done.1
  303.5 2.2 fusion.41
  305.8 0.0 all-reduce.8.cloned.1.call-update
  305.8 0.0 all-reduce.10.cloned.1.call-start
  305.9 5.5 fusion.15
  311.4 0.0 all-reduce.10.cloned.1.call-update
  311.4 60.1 %all-reduce.8.cloned.1.call-done = f32[512,256]{1,0:T(8,128)} async-done(((f32[512,256]{1,0:T(8,128)}), f32[512,256]{1,0:T(8,128)}) %all-reduce.8.cloned.1.call-update) | async-done | bytes 524304 | tf_op jit(solution)/shard_map/psum | solution.py:101
  371.5 1.3 multiply_reduce_fusion.2
  372.8 1.2 divide_convert_fusion
  374.0 4.1 gather_fusion
  378.1 0.2 gather.11
  378.2 1.0 broadcast_select_fusion
  379.2 15.6 %all-to-all-start.2 = ((bf16[64,15,256]{2,1,0:T(8,128)(2,1)}), bf16[64,15,256]{2,1,0:T(8,128)(2,1)S(1)}, u32[]{:S(2)}, u32[]{:S(2)}) async-start(bf16[64,15,256]{2,1,0:T(8,128)(2,1)} %broadcast_select_fusion), calls=%async_computation.2 | async-start | bytes 1048576 | tf_op jit(solution)/shard_map/all_to_all | solution.py:118
  395.5 0.6 divide_subtract_fusion
  396.1 37.8 %all-to-all-done.2 = bf16[64,15,256]{2,1,0:T(8,128)(2,1)S(1)} async-done(((bf16[64,15,256]{2,1,0:T(8,128)(2,1)}), bf16[64,15,256]{2,1,0:T(8,128)(2,1)S(1)}, u32[]{:S(2)}, u32[]{:S(2)}) %all-to-all-start.2) | async-done | bytes 491552 | tf_op jit(solution)/shard_map/all_to_all | solution.py:118
  433.9 0.2 reshape.272
  434.1 5.6 gather_fusion.1
  439.7 1.2 bitcast_select_fusion
  440.8 246.4 %all-reduce.10.cloned.1.call-done = f32[256,4096]{1,0:T(8,128)} async-done(((f32[256,4096]{1,0:T(8,128)}), f32[256,4096]{1,0:T(8,128)}) %all-reduce.10.cloned.1.call-update) | async-done | bytes 4194320
  687.3 1.5 constant_dynamic-slice_fusion
  (17 shorter events, 0.1 us)
Async XLA Ops:
  7.2 246.6 %copy-start = (bf16[256,4096]{1,0:T(8,128)(2,1)S(1)}, bf16[256,4096]{1,0:T(8,128)(2,1)}, u32[]{:S(2)}) copy-start(bf16[256,4096]{1,0:T(8,128)(2,1)} %param.12) | copy-start | bytes 6291460
  178.6 39.4 %all-to-all-start = ((bf16[64,15,256]{2,1,0:T(8,128)(2,1)}), bf16[64,15,256]{2,1,0:T(8,128)(2,1)S(1)}, u32[]{:S(2)}, u32[]{:S(2)}) async-start(bf16[64,15,256]{2,1,0:T(8,128)(2,1)} %reshape.268), calls=%async_computation | async-start | bytes 1048576 | tf_op jit(solution)/shard_map/all_to_all | solution.py:51
  185.4 73.0 %copy-start.2 = (f32[4096]{0:T(1024)S(1)}, f32[4096]{0:T(1024)}, u32[]{:S(2)}) copy-start(f32[4096]{0:T(1024)} %param.13) | copy-start | bytes 49156
  218.0 28.8 %all-to-all-start.1 = ((bf16[64,15,256]{2,1,0:T(8,128)(2,1)}), bf16[64,15,256]{2,1,0:T(8,128)(2,1)S(1)}, u32[]{:S(2)}, u32[]{:S(2)}) async-start(bf16[64,15,256]{2,1,0:T(8,128)(2,1)} %reshape.270), calls=%async_computation.1 | async-start | bytes 1048576 | tf_op jit(solution)/shard_map/all_to_all | solution.py:52
  223.9 147.6 %all-reduce.8.cloned.1.call-start = ((), (), s32[]{:S(2)}) async-start(), calls=%async_computation.3 | async-start | bytes 1048576 | tf_op jit(solution)/shard_map/psum | solution.py:101
  301.6 2.0 copy-start.1
  305.8 381.4 %all-reduce.10.cloned.1.call-start = ((), (), s32[]{:S(2)}) async-start(), calls=%async_computation.4 | async-start | bytes 8388608
  379.2 54.7 %all-to-all-start.2 = ((bf16[64,15,256]{2,1,0:T(8,128)(2,1)}), bf16[64,15,256]{2,1,0:T(8,128)(2,1)S(1)}, u32[]{:S(2)}, u32[]{:S(2)}) async-start(bf16[64,15,256]{2,1,0:T(8,128)(2,1)} %broadcast_select_fusion), calls=%async_computation.2 | async-start | bytes 1048576 | tf_op jit(solution)/shard_map/all_to_all | solution.py:118
Sparse Core Ops, SparseCore 0:
  305.9 65.4 all-reduce.7
  375.4 311.7 all-reduce.9
where the time goes:
time: 696 us
  waiting for transfers between devices  375 us (54%)
  blocking collectives  171 us (25%)
  local copies, waits for them, and re-layouts  57.8 us (8%)
  other arithmetic  29.7 us (4%)
  starting transfers between devices  28.3 us (4%)
  between operations  17.1 us (2%)
  matrix products  16.9 us (2%)
    unnamed x3, waiting for transfers between devices  246 us
    unnamed x1, blocking collectives  150 us
    psum x1, waiting for transfers between devices, on_device(): unit_grad = lax.psum(proto_part, 'proto')  60.1 us
    all_to_all x1, waiting for transfers between devices, on_device(): lax.all_to_all(back_rows, 'tok', split_axis=0, concat_axis=0, tiled=True)  37.8 us
    scatter x2, local copies, waits for them, and re-layouts, pack_rows(): buffer = jnp.zeros((slot_total, source.shape[1]), source.dtype).at[send_p...  21.3 us
    all_to_all x1, waiting for transfers between devices, on_device(): lax.all_to_all(pack_rows(student_tokens), 'tok', split_axis=0, concat_axi...  21 us
    all_to_all x1, starting transfers between devices, on_device(): lax.all_to_all(back_rows, 'tok', split_axis=0, concat_axis=0, tiled=True)  15.6 us
  transfers between devices with their start and end apart: 5, of which 5 were waited for; matrix products, arithmetic and copies ran while one was open for 7% of the time, Pallas kernels for 0%

commit v1 on v0

v1 whole, which is shorter than its diff:
```python
import jax
import jax.numpy as jnp
from jax import lax
from jax.experimental import pallas as pl
from jax.experimental.pallas import tpu as pltpu
from jax.sharding import PartitionSpec as P

MESH = pl.DeviceIdType.MESH
F32, BF16, I32 = jnp.float32, jnp.bfloat16, jnp.int32

NX, NZ, NY, NC = 4, 16, 4, 2
TOK = NX * NZ
D = 256
SEQ = 1568
CAP = 960
PAD = 1024
LOCAL = 4096
CHUNKS = 4
LANES = LOCAL // CHUNKS
TILE = 192
TILES = CAP // TILE
GROUP = 16
OUT = 512

LOG2E = 1.4426950408889634
LN2 = 0.6931471805599453
K_S = LOG2E / 0.1
K_U = LOG2E / 0.07

NT = (((1,), (1,)), ((), ()))


def lane_parts(values):
    return [values[:, j * 128 : (j + 1) * 128] for j in range(values.shape[1] // 128)]


def tree(op, parts):
    while len(parts) > 1:
        parts = [op(*parts[i : i + 2]) if i + 1 < len(parts) else parts[i] for i in range(0, len(parts), 2)]
    return parts[0]


def forward_kernel(
    student, teacher, mask, cot, protos, center,
    rows_out, xh_out, yh_out, xt_out, rank_out, stats_out,
    rank_row, dots, targets, peak_s, sum_s, peak_u, sum_u, cross,
):
    flags = mask[...].astype(F32)
    blocks = [flags[:, b * 128 : (b + 1) * 128] for b in range(SEQ // 128)]
    tail = SEQ % 128
    blocks.append(jnp.concatenate([flags[:, SEQ - tail :], jnp.zeros((1, 128 - tail), F32)], axis=1))
    blocks.append(jnp.zeros((16 - len(blocks), 128), F32))
    table = jnp.concatenate(blocks, axis=0)
    half = table.astype(BF16)
    row_i = lax.broadcasted_iota(I32, (128, 128), 0)
    col_i = lax.broadcasted_iota(I32, (128, 128), 1)
    upto = jnp.where(row_i <= col_i, 1.0, 0.0).astype(BF16)
    inside = jnp.dot(half, upto, preferred_element_type=F32)
    totals = jnp.dot(half, jnp.ones((128, 128), BF16), preferred_element_type=F32)
    before_r = lax.broadcasted_iota(I32, (16, 16), 0)
    before_c = lax.broadcasted_iota(I32, (16, 16), 1)
    before = jnp.where(before_c < before_r, 1.0, 0.0).astype(BF16)
    ahead = jnp.dot(before, totals.astype(BF16), preferred_element_type=F32)
    rank = jnp.where(table > 0.5, inside + ahead - 1.0, -1.0)
    rank_out[...] = rank
    for b in range(13):
        rank_row[:, b * 128 : (b + 1) * 128] = rank[b : b + 1, :]
    count = jnp.sum(jnp.sum(totals[:, 0:1], axis=0, keepdims=True), axis=1, keepdims=True)

    def compact(t, carry):
        at = pl.ds(pl.multiple_of(t * TILE, TILE), TILE)
        place = lax.broadcasted_iota(I32, (TILE, SEQ), 0) + t * TILE
        pick = jnp.where(rank_row[:, :SEQ] == place.astype(F32), 1.0, 0.0).astype(BF16)
        for source, unit_out in ((student, xh_out), (teacher, yh_out)):
            got = jnp.dot(pick, source[...], preferred_element_type=F32)
            length = jnp.sqrt(jnp.sum(got * got, axis=1, keepdims=True) + 1e-6)
            unit_out[at, :] = (got / length).astype(BF16)
            if unit_out is xh_out:
                rows_out[at, :] = got.astype(BF16)
        return carry

    lax.fori_loop(0, TILES, compact, 0)
    rows_out[CAP:, :] = jnp.zeros((PAD - CAP, D), BF16)

    line = lax.broadcasted_iota(I32, (D, D), 0)
    feature = lax.broadcasted_iota(I32, (D, D), 1)
    wanted = ((line >> 2) & (NZ - 1)) * 16 + (line >> 6) * 4 + (line & 3)
    order = jnp.where(feature == wanted, 1.0, 0.0).astype(BF16)
    xt_out[:, :CAP] = lax.dot_general(order, xh_out[...], NT, preferred_element_type=F32).astype(BF16)
    xt_out[:, CAP:] = jnp.zeros((D, PAD - CAP), BF16)

    for n in range(CHUNKS):
        cols = slice(n * LANES, (n + 1) * LANES)
        shift = lane_parts(center[:, cols] * K_U)

        def tile(t, carry, n=n, cols=cols, shift=shift):
            at = pl.multiple_of(t * TILE, TILE)
            rows = pl.ds(at, TILE)
            dots[...] = jnp.dot(xh_out[rows, :], protos[:, cols], preferred_element_type=F32)
            targets[...] = jnp.dot(yh_out[rows, :], protos[:, cols], preferred_element_type=F32)
            for k in range(TILE // GROUP):
                here = slice(k * GROUP, (k + 1) * GROUP)
                there = pl.ds(pl.multiple_of(at + k * GROUP, GROUP), GROUP)
                s = lane_parts(dots[here, :] * K_S)
                u = [a * K_U - b for a, b in zip(lane_parts(targets[here, :]), shift)]
                top_s = tree(jnp.maximum, s)
                top_u = tree(jnp.maximum, u)
                if n:
                    old_s, old_u = peak_s[there, :], peak_u[there, :]
                    top_s = jnp.maximum(top_s, old_s)
                    top_u = jnp.maximum(top_u, old_u)
                add_s = tree(jnp.add, [jnp.exp2(a - top_s) for a in s])
                tilted = [jnp.exp2(a - top_u) for a in u]
                add_u = tree(jnp.add, tilted)
                add_x = tree(jnp.add, [a * b for a, b in zip(tilted, s)])
                if n:
                    fade_u = jnp.exp2(old_u - top_u)
                    add_s = add_s + sum_s[there, :] * jnp.exp2(old_s - top_s)
                    add_u = add_u + sum_u[there, :] * fade_u
                    add_x = add_x + cross[there, :] * fade_u
                peak_s[there, :] = top_s
                peak_u[there, :] = top_u
                sum_s[there, :] = add_s
                sum_u[there, :] = add_u
                cross[there, :] = add_x
            return carry

        lax.fori_loop(0, TILES, tile, 0)

    weight = cot[...] / count
    lane = lax.broadcasted_iota(I32, (TILE, 128), 1)

    def finish(t, carry):
        at = pl.ds(pl.multiple_of(t * TILE, TILE), TILE)
        top_s = jnp.max(peak_s[at, :], axis=1, keepdims=True)
        top_u = jnp.max(peak_u[at, :], axis=1, keepdims=True)
        fade_u = jnp.exp2(peak_u[at, :] - top_u)
        all_s = jnp.sum(sum_s[at, :] * jnp.exp2(peak_s[at, :] - top_s), axis=1, keepdims=True)
        all_u = jnp.sum(sum_u[at, :] * fade_u, axis=1, keepdims=True)
        all_x = jnp.sum(cross[at, :] * fade_u, axis=1, keepdims=True)
        packed = jnp.where(lane == 0, top_s, jnp.where(lane == 1, all_s, jnp.where(lane == 2, top_u, jnp.where(lane == 3, all_u, all_x))))
        peak_s[at, :] = packed
        return carry

    lax.fori_loop(0, TILES, finish, 0)
    peak_s[CAP:, :] = jnp.ones((PAD - CAP, 128), F32)
    line8 = lax.broadcasted_iota(I32, (8, 128), 0)
    for b in range(PAD // 128):
        turned = jnp.transpose(peak_s[b * 128 : (b + 1) * 128, :])[0:8, :]
        turned = jnp.where(line8 == 5, weight, jnp.where(line8 == 6, count, turned))
        stats_out[:, b * 128 : (b + 1) * 128] = turned


def backward_kernel(
    stats, xh, yh, xt, rows_in, protos, center,
    grad_out, feat_out, loss_out,
    stat_got, shift_s, shift_u, dots, targets, grads, du, part, own,
    x_send, x_got, z_send, z_got, f_send, f_got, f_all, losses,
    stat_ss, stat_rs, lx_ss, lx_rs, lz_ss, lz_rs, x_ss, x_rs, z_ss, z_rs, f_ss, f_rs, g_ss, g_rs,
):
    tok = lax.axis_index("tok")
    pro = lax.axis_index("proto")
    z, x = tok // NX, lax.rem(tok, NX)
    y, c = pro // NC, lax.rem(pro, NC)
    x_peers = [lax.rem(x + d, NX) for d in range(1, NX)]
    z_peers = [lax.rem(z + d, NZ) for d in range(1, NZ)]
    p_peers = [lax.rem(y + d // NC, NY) * NC + lax.rem(c + d % NC, NC) for d in range(1, NY * NC)]
    x_ids = [(z * NX + q, pro) for q in x_peers]
    z_ids = [(q * NX + x, pro) for q in z_peers]
    p_ids = [(tok, q) for q in p_peers]

    barrier = pltpu.get_barrier_semaphore()
    everyone = x_ids + z_ids + p_ids
    for q in everyone:
        pl.semaphore_signal(barrier, inc=1, device_id=q, device_id_type=MESH)
    pl.semaphore_wait(barrier, len(everyone))

    def send(src, dst, ss, rs, device):
        copy = pltpu.make_async_remote_copy(
            src_ref=src, dst_ref=dst, send_sem=ss, recv_sem=rs, device_id=device, device_id_type=MESH
        )
        copy.start()
        return copy

    stat_copies = [
        send(stats, stat_got.at[i], stat_ss.at[i], stat_rs.at[i], q) for i, q in enumerate(p_ids)
    ]
    grads[CAP:, :] = jnp.zeros((PAD - CAP, LANES), BF16)
    for copy in stat_copies:
        copy.wait_recv()
    mine = stats[...]
    tables = [mine] + [stat_got[i] for i in range(NY * NC - 1)]
    top_s = tree(jnp.maximum, [a[0:1] for a in tables])
    top_u = tree(jnp.maximum, [a[2:3] for a in tables])
    all_s = tree(jnp.add, [a[1:2] * jnp.exp2(a[0:1] - top_s) for a in tables])
    fades = [jnp.exp2(a[2:3] - top_u) for a in tables]
    all_u = tree(jnp.add, [a[3:4] * f for a, f in zip(tables, fades)])
    all_x = tree(jnp.add, [a[4:5] * f for a, f in zip(tables, fades)])
    lse_s = top_s + jnp.log2(all_s)
    lse_u = top_u + jnp.log2(all_u)
    loss = (lse_s - all_x / all_u) * LN2
    scale = jnp.log2(mine[5:6] * 10.0)
    for b in range(PAD // 128):
        cols = slice(b * 128, (b + 1) * 128)
        shift_s[cols, :] = jnp.transpose(jnp.broadcast_to((lse_s - scale)[:, cols], (128, 128)))
        shift_u[cols, :] = jnp.transpose(jnp.broadcast_to((lse_u - scale)[:, cols], (128, 128)))

    sheet = jnp.concatenate([loss[:, b * 128 : (b + 1) * 128] for b in range(PAD // 128)], axis=0)
    line = lax.broadcasted_iota(I32, (8, 128), 0)
    lane = lax.broadcasted_iota(I32, (8, 128), 1)
    sheet = jnp.where((line == 7) & (lane == 127), mine[6:7, 0:128], sheet)
    losses[tok] = sheet
    lx_copies = [
        send(losses.at[tok], losses.at[tok], lx_ss.at[i], lx_rs.at[i], q) for i, q in enumerate(x_ids)
    ]

    x_copies, z_copies = [], []

    def along_x(n):
        for copy in x_copies[n]:
            copy.wait_recv()
        total = own[n]
        for i in range(NX - 1):
            total = total + x_got[n, i].astype(F32)
        for q in range(NZ):
            piece = jnp.concatenate(
                [total[4 * q : 4 * q + 4, j * 256 : (j + 1) * 256] for j in range(4)], axis=0
            )
            z_send[n, q] = piece.astype(BF16)
        z_copies.append(
            [
                send(z_send.at[n, q], z_got.at[n, i], z_ss.at[n, i], z_rs.at[n, i], device)
                for i, (q, device) in enumerate(zip(z_peers, z_ids))
            ]
        )

    for n in range(CHUNKS):
        cols = slice(n * LANES, (n + 1) * LANES)
        shift = lane_parts(center[:, cols] * K_U)

        def tile(t, carry, n=n, cols=cols, shift=shift):
            at = pl.multiple_of(t * TILE, TILE)
            rows = pl.ds(at, TILE)
            dots[...] = jnp.dot(xh[rows, :], protos[:, cols], preferred_element_type=F32)
            targets[...] = jnp.dot(yh[rows, :], protos[:, cols], preferred_element_type=F32)
            for k in range(TILE // GROUP):
                here = slice(k * GROUP, (k + 1) * GROUP)
                there = pl.ds(pl.multiple_of(at + k * GROUP, GROUP), GROUP)
                less_s, less_u = shift_s[there, :], shift_u[there, :]
                s = lane_parts(dots[here, :])
                u = lane_parts(targets[here, :])
                for j in range(LANES // 128):
                    g = jnp.exp2(s[j] * K_S - less_s) - jnp.exp2(u[j] * K_U - (less_u + shift[j]))
                    grads[there, j * 128 : (j + 1) * 128] = g.astype(BF16)
            add = lax.dot_general(grads[rows, :], protos[:, cols], NT, preferred_element_type=F32)
            if n:
                add = add + du[rows, :]
            du[rows, :] = add
            return carry

        lax.fori_loop(0, TILES, tile, 0)
        for j in range(LANES // 256):
            lanes = slice(j * 256, (j + 1) * 256)
            piece = jnp.dot(xt[...], grads[:, lanes], preferred_element_type=F32)
            part[:, lanes] = piece
            x_send[n, :, lanes] = piece.astype(BF16)
        x_copies.append(
            [
                send(
                    x_send.at[n, pl.ds(pl.multiple_of(q * 64, 64), 64)],
                    x_got.at[n, i], x_ss.at[n, i], x_rs.at[n, i], device,
                )
                for i, (q, device) in enumerate(zip(x_peers, x_ids))
            ]
        )
        own[n] = part[pl.ds(pl.multiple_of(x * 64, 64), 64), :]
        if n == 0:
            for copy in lx_copies:
                copy.wait_recv()
            row = pl.ds(pl.multiple_of(z * NX, NX), NX)
            lz_copies = [
                send(losses.at[row], losses.at[row], lz_ss.at[i], lz_rs.at[i], q)
                for i, q in enumerate(z_ids)
            ]
        else:
            if n == CHUNKS - 1:
                for q in range(NY * NC):
                    size = min(128, CAP - q * 128)
                    f_send[q, :size, :] = du[q * 128 : q * 128 + size, :].astype(BF16)
                    if size < 128:
                        f_send[q, size:, :] = jnp.zeros((128 - size, D), BF16)
                f_copies = [
                    send(f_send.at[q], f_got.at[i], f_ss.at[i], f_rs.at[i], device)
                    for i, (q, device) in enumerate(zip(p_peers, p_ids))
                ]
            along_x(n - 1)

    for copy in f_copies:
        copy.wait_recv()
    total = f_send[pro].astype(F32)
    for i in range(NY * NC - 1):
        total = total + f_got[i].astype(F32)
    rows = rows_in[pl.ds(pl.multiple_of(pro * 128, 128), 128), :].astype(F32)
    length = jnp.sqrt(jnp.sum(rows * rows, axis=1, keepdims=True) + 1e-6)
    unit = rows / length
    total = (total - unit * jnp.sum(unit * total, axis=1, keepdims=True)) / length
    f_all[pro] = total.astype(BF16)
    g_copies = [
        send(f_all.at[pro], f_all.at[pro], g_ss.at[i], g_rs.at[i], q) for i, q in enumerate(p_ids)
    ]

    along_x(CHUNKS - 1)
    for copy in lz_copies:
        copy.wait_recv()
    loss_out[...] = losses[...]
    for copy in g_copies:
        copy.wait_recv()
    for q in range(NY * NC):
        feat_out[q * 128 : (q + 1) * 128, :] = f_all[q]
    for n in range(CHUNKS):
        for copy in z_copies[n]:
            copy.wait_recv()
        total = z_send[n, z].astype(F32)
        for i in range(NZ - 1):
            total = total + z_got[n, i].astype(F32)
        for j in range(4):
            at = n * LANES + j * 256
            grad_out[:, at : at + 256] = total[j * 4 : j * 4 + 4, :]
    for copy in stat_copies + lx_copies + lz_copies + f_copies + g_copies:
        copy.wait_send()
    for n in range(CHUNKS):
        for copy in x_copies[n] + z_copies[n]:
            copy.wait_send()


def place_kernel(rank, feat, losses, perm, token_out, loss_out):
    turned = jnp.transpose(jnp.concatenate([rank[...], jnp.zeros((112, 128), F32)], axis=0))
    spot = lax.broadcasted_iota(I32, (128, PAD), 1).astype(F32)
    for b in range(13):
        size = min(128, SEQ - b * 128)
        pick = jnp.where(turned[:size, b : b + 1] == spot[:size], 1.0, 0.0).astype(BF16)
        token_out[b * 128 : b * 128 + size, :] = jnp.dot(
            pick, feat[...], preferred_element_type=F32
        ).astype(BF16)

    me = lax.axis_index("tok")
    table = losses[...]
    lane2 = lax.broadcasted_iota(I32, (TOK, 128), 1)
    counts = jnp.sum(jnp.where(lane2 == 127, table[:, 7, :], 0.0), axis=1, keepdims=True)
    counts = jnp.broadcast_to(counts, (TOK, 128))
    r_i = lax.broadcasted_iota(I32, (TOK, TOK), 0)
    c_i = lax.broadcasted_iota(I32, (TOK, TOK), 1)
    offsets = jnp.dot(
        jnp.where(c_i < r_i, 1.0, 0.0), counts, preferred_element_type=F32, precision=lax.Precision.HIGHEST
    )
    offsets = jnp.round(offsets).astype(I32)
    sizes = counts.astype(I32)
    slots = lax.broadcasted_iota(I32, (1, TOK), 1)
    slot = jnp.sum(jnp.where(perm[...] == me, slots, 0), axis=1, keepdims=True)
    first = (slot - offsets) & 63
    shape = (TOK, 8, 128)
    first3 = jnp.broadcast_to(first[:, None, :], shape)
    off3 = jnp.broadcast_to(offsets[:, None, :], shape)
    size3 = jnp.broadcast_to(sizes[:, None, :], shape)
    lane3 = lax.broadcasted_iota(I32, shape, 2)
    index3 = lax.broadcasted_iota(I32, shape, 1) * 128 + first3
    places = lax.broadcasted_iota(I32, (TOK * 8, 128), 1)
    for q in range(OUT // 128):
        acc = jnp.zeros((1, 128), F32)
        for part in range(2):
            index = index3 + part * 64
            value = jnp.sum(
                jnp.where((lane3 == first3 + part * 64) & (index < size3), table, 0.0), axis=2, keepdims=True
            )
            value = jnp.broadcast_to(value, shape).reshape(TOK * 8, 128)
            goal = ((off3 + index) >> 6).reshape(TOK * 8, 128)
            acc = acc + jnp.sum(jnp.where(goal == places + q * 128, value, 0.0), axis=0, keepdims=True)
        loss_out[:, q * 128 : (q + 1) * 128] = acc


def vmem(count):
    return [pl.BlockSpec(memory_space=pltpu.VMEM)] * count


def on_device(student, teacher, mask, perm, cot, protos, center):
    shape = jax.ShapeDtypeStruct
    center = center.reshape(1, LOCAL)
    rows, xh, yh, xt, rank, stats = pl.pallas_call(
        forward_kernel,
        out_shape=(
            shape((PAD, D), BF16), shape((CAP, D), BF16), shape((CAP, D), BF16),
            shape((D, PAD), BF16), shape((16, 128), F32), shape((8, PAD), F32),
        ),
        in_specs=vmem(6),
        out_specs=tuple(vmem(6)),
        scratch_shapes=[
            pltpu.VMEM((1, 13 * 128), F32),
            pltpu.VMEM((TILE, LANES), F32),
            pltpu.VMEM((TILE, LANES), F32),
            pltpu.VMEM((PAD, 128), F32),
        ] + [pltpu.VMEM((CAP, 128), F32)] * 4,
        compiler_params=pltpu.CompilerParams(vmem_limit_bytes=48 << 20),
        name="forward",
    )(student[0], teacher[0], mask, cot.reshape(1, 1), protos, center)

    dma = lambda *s: pltpu.SemaphoreType.DMA(s)
    peers = NY * NC - 1
    grad, feat, losses = pl.pallas_call(
        backward_kernel,
        out_shape=(shape((4, LOCAL), F32), shape((PAD, D), BF16), shape((TOK, 8, 128), F32)),
        in_specs=vmem(7),
        out_specs=tuple(vmem(3)),
        scratch_shapes=[
            pltpu.VMEM((peers, 8, PAD), F32),
            pltpu.VMEM((PAD, 128), F32),
            pltpu.VMEM((PAD, 128), F32),
            pltpu.VMEM((TILE, LANES), F32),
            pltpu.VMEM((TILE, LANES), F32),
            pltpu.VMEM((PAD, LANES), BF16),
            pltpu.VMEM((CAP, D), F32),
            pltpu.VMEM((D, LANES), F32),
            pltpu.VMEM((CHUNKS, 64, LANES), F32),
            pltpu.VMEM((CHUNKS, D, LANES), BF16),
            pltpu.VMEM((CHUNKS, NX - 1, 64, LANES), BF16),
            pltpu.VMEM((CHUNKS, NZ, 16, 256), BF16),
            pltpu.VMEM((CHUNKS, NZ - 1, 16, 256), BF16),
            pltpu.VMEM((NY * NC, 128, D), BF16),
            pltpu.VMEM((peers, 128, D), BF16),
            pltpu.VMEM((NY * NC, 128, D), BF16),
            pltpu.VMEM((TOK, 8, 128), F32),
            dma(peers), dma(peers),
            dma(NX - 1), dma(NX - 1),
            dma(NZ - 1), dma(NZ - 1),
            dma(CHUNKS, NX - 1), dma(CHUNKS, NX - 1),
            dma(CHUNKS, NZ - 1), dma(CHUNKS, NZ - 1),
            dma(peers), dma(peers),
            dma(peers), dma(peers),
        ],
        compiler_params=pltpu.CompilerParams(
            collective_id=1, has_side_effects=True, vmem_limit_bytes=48 << 20
        ),
        name="backward",
    )(stats, xh, yh, xt, rows, protos, center)

    tokens, row_loss = pl.pallas_call(
        place_kernel,
        out_shape=(shape((SEQ, D), BF16), shape((1, OUT), F32)),
        in_specs=vmem(4),
        out_specs=tuple(vmem(2)),
        compiler_params=pltpu.CompilerParams(vmem_limit_bytes=48 << 20),
        name="place",
    )(rank, feat, losses, perm.reshape(1, TOK))
    return tokens[None], grad, row_loss.reshape(OUT)


def solution(mesh):
    in_specs = (
        P("tok", None, None),
        P("tok", None, None),
        P("tok", None),
        P(),
        P("tok"),
        P(None, "proto"),
        P("proto"),
    )
    out_specs = (P("tok", None, None), P("tok", "proto"), P("tok"))
    return jax.shard_map(
        on_device, mesh=mesh, in_specs=in_specs, out_specs=out_specs, check_vma=False
    )
```

time: 696 us -> 93.5 us (0.13)
  the two profiles are of different devices: /device:TPU:16 before, /device:TPU:1 now
where the time goes in v1:
time: 93.5 us; the launch traced here: 93.2 us
  Pallas kernels  86 us (92%)
  local copies, waits for them, and re-layouts  5.91 us (6%)
  between operations  1.31 us (1%)
    pallas_call x1, Pallas kernels, on_device(): pl.pallas_call(backward_kernel, out_shape=(shape((4, LOCAL), F32), shape(...  65.3 us
    pallas_call x1, Pallas kernels, on_device(): pl.pallas_call(forward_kernel, out_shape=(shape((PAD, D), BF16), shape((C...  18.3 us
    unnamed x15, local copies, waits for them, and re-layouts  5.91 us
    pallas_call x1, Pallas kernels, on_device(): pl.pallas_call(place_kernel, out_shape=(shape((SEQ, D), BF16), shape((1,...  2.36 us

profile of v1, /device:TPU:1, one launch (start us, length us, event | category | flops | bytes accessed | tf_op | source)
XLA Modules:
  0.0 93.2 jit_solution(7618432294148852150)
XLA Ops:
  1.3 0.0 copy-start
  1.3 1.6 %copy-done = bf16[256,4096]{1,0:T(8,128)(2,1)S(1)} copy-done((bf16[256,4096]{1,0:T(8,128)(2,1)S(1)}, bf16[256,4096]{1,0:T(8,128)(2,1)}, u32[]{:S(2)}) %copy-start) | copy-done | bytes 2097176
  2.9 0.0 copy-start.2
  2.9 1.1 %copy-done.2 = bf16[1,1568,256]{2,1,0:T(8,128)(2,1)S(1)} copy-done((bf16[1,1568,256]{2,1,0:T(8,128)(2,1)S(1)}, bf16[1,1568,256]{2,1,0:T(8,128)(2,1)}, u32[]{:S(2)}) %copy-start.2) | copy-done | bytes 802840
  4.0 0.0 copy-start.3
  4.0 1.1 %copy-done.3 = bf16[1,1568,256]{2,1,0:T(8,128)(2,1)S(1)} copy-done((bf16[1,1568,256]{2,1,0:T(8,128)(2,1)S(1)}, bf16[1,1568,256]{2,1,0:T(8,128)(2,1)}, u32[]{:S(2)}) %copy-start.3) | copy-done | bytes 802840
  5.1 0.0 copy-start.4
  5.2 0.7 copy-done.4
  5.9 0.0 copy-start.5
  5.9 0.7 copy-done.5
  6.6 0.0 copy-start.1
  6.6 18.3 %forward.1 = (bf16[1024,256]{1,0:T(8,128)(2,1)S(1)}, bf16[960,256]{1,0:T(8,128)(2,1)S(1)}, bf16[960,256]{1,0:T(8,128)(2,1)S(1)}, bf16[256,1024]{1,0:T(8,128)(2,1...) custom-call(bf16[1568,256]{1,0:T(8,128)(2,1)S(1)} %bitcast.8, bf16[1568,256]{1,0:T(8,128)(2,1)S(1)} %bitcast.9, ...), custom_call_target="tpu_custom_call" | custom-call | tf_op jit(solution)/shard_map/forward/pallas_call | solution.py:388
  24.9 0.0 copy-start.6
  24.9 0.0 copy-done.1
  24.9 65.3 %backward.1 = (f32[4,4096]{1,0:T(4,128)S(1)}, bf16[1024,256]{1,0:T(8,128)(2,1)S(1)}, f32[64,8,128]{2,1,0:T(8,128)S(1)}) custom-call(f32[8,1024]{1,0:T(8,128)S(1)} %get-tuple-element.15.stats, bf16[960,256]{1,0:T(8,128)(2,1)S(1)} %get-tuple-element.16.xh, bf16[960,256]{1,0:T(8,128)(2,1)S(1)} %get-tuple-element.17.yh, ...), custom_call_target="tpu_custom_call" | custom-call | tf_op jit(solution)/shard_map/backward/pallas_call | solution.py:408
  90.2 0.0 copy-done.6
  90.2 2.4 %place.1 = (bf16[1568,256]{1,0:T(8,128)(2,1)}, f32[1,512]{1,0:T(1,128)}) custom-call(f32[16,128]{1,0:T(8,128)S(1)} %get-tuple-element.14.rank, bf16[1024,256]{1,0:T(8,128)(2,1)S(1)} %get-tuple-element.20.feat, f32[64,8,128]{2,1,0:T(8,128)S(1)} %get-tuple-element.21.losses, s32[1,64]{1,0:T(1,128)S(1)} %bitcast.12), custom_call_target="tpu_custom_call" | custom-call | tf_op jit(solution)/shard_map/place/pallas_call | solution.py:445
  92.6 0.6 copy.12
Async XLA Ops:
  1.3 1.6 %copy-start = (bf16[256,4096]{1,0:T(8,128)(2,1)S(1)}, bf16[256,4096]{1,0:T(8,128)(2,1)}, u32[]{:S(2)}) copy-start(bf16[256,4096]{1,0:T(8,128)(2,1)} %protos.3) | copy-start | bytes 6291460
  2.9 1.1 %copy-start.2 = (bf16[1,1568,256]{2,1,0:T(8,128)(2,1)S(1)}, bf16[1,1568,256]{2,1,0:T(8,128)(2,1)}, u32[]{:S(2)}) copy-start(bf16[1,1568,256]{2,1,0:T(8,128)(2,1)} %param.7) | copy-start | bytes 2408452
  4.0 1.1 %copy-start.3 = (bf16[1,1568,256]{2,1,0:T(8,128)(2,1)S(1)}, bf16[1,1568,256]{2,1,0:T(8,128)(2,1)}, u32[]{:S(2)}) copy-start(bf16[1,1568,256]{2,1,0:T(8,128)(2,1)} %param.8) | copy-start | bytes 2408452
  5.1 0.7 copy-start.4
  5.9 0.7 copy-start.5
  6.6 18.3 %copy-start.1 = (bf16[256,4096]{1,0:T(8,128)(2,1)S(1)}, bf16[256,4096]{1,0:T(8,128)(2,1)}, u32[]{:S(2)}) copy-start(bf16[256,4096]{1,0:T(8,128)(2,1)} %protos.3) | copy-start | bytes 6291460
  24.9 65.3 %copy-start.6 = (s32[64]{0:T(128)S(1)}, s32[64]{0:T(128)}, u32[]{:S(2)}) copy-start(s32[64]{0:T(128)} %param.10) | copy-start | bytes 772

commit v2 on v1

v2 whole, which is shorter than its diff:
```python
import jax
import jax.numpy as jnp
from jax import lax
from jax.experimental import pallas as pl
from jax.experimental.pallas import tpu as pltpu
from jax.sharding import PartitionSpec as P

MESH = pl.DeviceIdType.MESH
F32, BF16, I32 = jnp.float32, jnp.bfloat16, jnp.int32

NX, NZ, NY, NC = 4, 16, 4, 2
TOK = NX * NZ
D = 256
SEQ = 1568
CAP = 960
PAD = 1024
LOCAL = 4096
WIDTHS = (512, 1024, 1024, 1024, 512)
STARTS = tuple(sum(WIDTHS[:n]) for n in range(len(WIDTHS)))
CHUNKS = len(WIDTHS)
LANES = max(WIDTHS)
TILE = 480
TILES = CAP // TILE
GROUP = 16
OUT = 512

LOG2E = 1.4426950408889634
LN2 = 0.6931471805599453
K_S = LOG2E / 0.1
K_U = LOG2E / 0.07

NT = (((1,), (1,)), ((), ()))


def lane_parts(values):
    return [values[:, j * 128 : (j + 1) * 128] for j in range(values.shape[1] // 128)]


def tree(op, parts):
    while len(parts) > 1:
        parts = [op(*parts[i : i + 2]) if i + 1 < len(parts) else parts[i] for i in range(0, len(parts), 2)]
    return parts[0]


def main_kernel(
    student_in, teacher_in, mask_in, cot, protos_in, center_in,
    grad_out, feat_out, loss_out, rank_out,
    student, teacher, mask, protos, center, in_sem, rank_row, rows_in, xh, yh, xt,
    dots_a, dots_b, dots_c, dots_d, dots_e, targets_a, targets_b, targets_c, targets_d, targets_e,
    peak_s, sum_s, peak_u, sum_u, cross, stats,
    stat_got, shift_s, shift_u, grads_a, grads_b, du, part, own,
    x_send, x_relay, x_sum, x_got, z_send, z_near, z_next, z_sum, z_own, z_got,
    f_send, f_pair, f_sum, f_got, f_all, losses,
    stat_ss, stat_rs, lx_ss, lx_rs, lz_ss, lz_rs, x_ss, x_rs, z_ss, z_rs, f_ss, f_rs,
):
    fetches = [
        pltpu.make_async_copy(a, b, in_sem.at[i])
        for i, (a, b) in enumerate(
            (
                (mask_in, mask), (student_in, student), (teacher_in, teacher),
                (protos_in, protos), (center_in, center),
            )
        )
    ]
    for copy in fetches:
        copy.start()
    dots = (dots_a, dots_b, dots_c, dots_d, dots_e)
    targets = (targets_a, targets_b, targets_c, targets_d, targets_e)
    grads = (grads_a, grads_b)

    tok = lax.axis_index("tok")
    pro = lax.axis_index("proto")
    z, x = tok // NX, lax.rem(tok, NX)
    y, c = pro // NC, lax.rem(pro, NC)
    z_high, z_low = z // 4, lax.rem(z, 4)
    p_peers = [lax.rem(y + d // NC, NY) * NC + lax.rem(c + d % NC, NC) for d in range(1, NY * NC)]
    p_ids = [(tok, q) for q in p_peers]

    pair = (tok, y * NC + 1 - c)

    def y_id(d):
        return (tok, lax.rem(y + d, NY) * NC + c)

    def x_id(d):
        return (z * NX + lax.rem(x + d + NX, NX), pro)

    def z_id(d):
        return (lax.rem(z + d + NZ, NZ) * NX + x, pro)

    barrier = pltpu.get_barrier_semaphore()
    everyone = [x_id(d) for d in (1, 2, 3)] + [z_id(d) for d in (1, -1, 2, -2, 4, -4, 8)] + p_ids
    for q in everyone:
        pl.semaphore_signal(barrier, inc=1, device_id=q, device_id_type=MESH)

    fetches[0].wait()
    flags = mask[...].astype(F32)
    blocks = [flags[:, b * 128 : (b + 1) * 128] for b in range(SEQ // 128)]
    tail = SEQ % 128
    blocks.append(jnp.concatenate([flags[:, SEQ - tail :], jnp.zeros((1, 128 - tail), F32)], axis=1))
    blocks.append(jnp.zeros((16 - len(blocks), 128), F32))
    table = jnp.concatenate(blocks, axis=0)
    half = table.astype(BF16)
    row_i = lax.broadcasted_iota(I32, (128, 128), 0)
    col_i = lax.broadcasted_iota(I32, (128, 128), 1)
    upto = jnp.where(row_i <= col_i, 1.0, 0.0).astype(BF16)
    inside = jnp.dot(half, upto, preferred_element_type=F32)
    totals = jnp.dot(half, jnp.ones((128, 128), BF16), preferred_element_type=F32)
    before_r = lax.broadcasted_iota(I32, (16, 16), 0)
    before_c = lax.broadcasted_iota(I32, (16, 16), 1)
    before = jnp.where(before_c < before_r, 1.0, 0.0).astype(BF16)
    ahead = jnp.dot(before, totals.astype(BF16), preferred_element_type=F32)
    rank = jnp.where(table > 0.5, inside + ahead - 1.0, -1.0)
    rank_out[...] = rank
    for b in range(13):
        rank_row[:, b * 128 : (b + 1) * 128] = rank[b : b + 1, :]
    count = jnp.sum(jnp.sum(totals[:, 0:1], axis=0, keepdims=True), axis=1, keepdims=True)

    fetches[1].wait()
    fetches[2].wait()

    def compact(t, carry):
        at = pl.ds(pl.multiple_of(t * TILE, TILE), TILE)
        place = lax.broadcasted_iota(I32, (TILE, SEQ), 0) + t * TILE
        pick = jnp.where(rank_row[:, :SEQ] == place.astype(F32), 1.0, 0.0).astype(BF16)
        for source, unit_out in ((student, xh), (teacher, yh)):
            got = jnp.dot(pick, source[...], preferred_element_type=F32)
            length = jnp.sqrt(jnp.sum(got * got, axis=1, keepdims=True) + 1e-6)
            unit_out[at, :] = (got / length).astype(BF16)
            if unit_out is xh:
                rows_in[at, :] = got.astype(BF16)
        return carry

    lax.fori_loop(0, TILES, compact, 0)
    rows_in[CAP:, :] = jnp.zeros((PAD - CAP, D), BF16)

    line = lax.broadcasted_iota(I32, (D, D), 0)
    feature = lax.broadcasted_iota(I32, (D, D), 1)
    wanted = ((line >> 2) & (NZ - 1)) * 16 + (line >> 6) * 4 + (line & 3)
    order = jnp.where(feature == wanted, 1.0, 0.0).astype(BF16)
    xt[:, :CAP] = lax.dot_general(order, xh[...], NT, preferred_element_type=F32).astype(BF16)
    xt[:, CAP:] = jnp.zeros((D, PAD - CAP), BF16)

    fetches[3].wait()
    fetches[4].wait()

    def columns(n):
        return slice(STARTS[n], STARTS[n] + WIDTHS[n])

    def scores(n, rows):
        dots[n][rows, :] = jnp.dot(xh[rows, :], protos[:, columns(n)], preferred_element_type=F32)
        targets[n][rows, :] = jnp.dot(yh[rows, :], protos[:, columns(n)], preferred_element_type=F32)

    def first(t, carry):
        scores(0, pl.ds(pl.multiple_of(t * TILE, TILE), TILE))
        return carry

    lax.fori_loop(0, TILES, first, 0)
    for n in range(CHUNKS):
        shift = lane_parts(center[:, columns(n)] * K_U)

        def gather(t, carry, n=n, shift=shift):
            at = pl.multiple_of(t * TILE, TILE)
            if n + 1 < CHUNKS:
                scores(n + 1, pl.ds(at, TILE))
            for k in range(TILE // GROUP):
                there = pl.ds(pl.multiple_of(at + k * GROUP, GROUP), GROUP)
                s = lane_parts(dots[n][there, :] * K_S)
                u = [a * K_U - b for a, b in zip(lane_parts(targets[n][there, :]), shift)]
                top_s = tree(jnp.maximum, s)
                top_u = tree(jnp.maximum, u)
                if n:
                    old_s, old_u = peak_s[there, :], peak_u[there, :]
                    top_s = jnp.maximum(top_s, old_s)
                    top_u = jnp.maximum(top_u, old_u)
                add_s = tree(jnp.add, [jnp.exp2(a - top_s) for a in s])
                tilted = [jnp.exp2(a - top_u) for a in u]
                add_u = tree(jnp.add, tilted)
                add_x = tree(jnp.add, [a * b for a, b in zip(tilted, s)])
                if n:
                    fade_u = jnp.exp2(old_u - top_u)
                    add_s = add_s + sum_s[there, :] * jnp.exp2(old_s - top_s)
                    add_u = add_u + sum_u[there, :] * fade_u
                    add_x = add_x + cross[there, :] * fade_u
                peak_s[there, :] = top_s
                peak_u[there, :] = top_u
                sum_s[there, :] = add_s
                sum_u[there, :] = add_u
                cross[there, :] = add_x
            return carry

        lax.fori_loop(0, TILES, gather, 0)

    weight = cot[...] / count
    lane = lax.broadcasted_iota(I32, (TILE, 128), 1)

    def merge(t, carry):
        at = pl.ds(pl.multiple_of(t * TILE, TILE), TILE)
        top_s = jnp.max(peak_s[at, :], axis=1, keepdims=True)
        top_u = jnp.max(peak_u[at, :], axis=1, keepdims=True)
        fade_u = jnp.exp2(peak_u[at, :] - top_u)
        all_s = jnp.sum(sum_s[at, :] * jnp.exp2(peak_s[at, :] - top_s), axis=1, keepdims=True)
        all_u = jnp.sum(sum_u[at, :] * fade_u, axis=1, keepdims=True)
        all_x = jnp.sum(cross[at, :] * fade_u, axis=1, keepdims=True)
        packed = jnp.where(lane == 0, top_s, jnp.where(lane == 1, all_s, jnp.where(lane == 2, top_u, jnp.where(lane == 3, all_u, all_x))))
        peak_s[at, :] = packed
        return carry

    lax.fori_loop(0, TILES, merge, 0)
    peak_s[CAP:, :] = jnp.ones((PAD - CAP, 128), F32)
    line8 = lax.broadcasted_iota(I32, (8, 128), 0)
    for b in range(PAD // 128):
        turned = jnp.transpose(peak_s[b * 128 : (b + 1) * 128, :])[0:8, :]
        turned = jnp.where(line8 == 5, weight, jnp.where(line8 == 6, count, turned))
        stats[:, b * 128 : (b + 1) * 128] = turned

    pl.semaphore_wait(barrier, len(everyone))

    def send(src, dst, ss, rs, device):
        copy = pltpu.make_async_remote_copy(
            src_ref=src, dst_ref=dst, send_sem=ss, recv_sem=rs, device_id=device, device_id_type=MESH
        )
        copy.start()
        return copy

    stat_copies = [
        send(stats, stat_got.at[i], stat_ss.at[i], stat_rs.at[i], q) for i, q in enumerate(p_ids)
    ]
    for ref in grads:
        ref[CAP:, :] = jnp.zeros((PAD - CAP, LANES), BF16)
    for copy in stat_copies:
        copy.wait_recv()
    mine = stats[...]
    tables = [mine] + [stat_got[i] for i in range(NY * NC - 1)]
    top_s = tree(jnp.maximum, [a[0:1] for a in tables])
    top_u = tree(jnp.maximum, [a[2:3] for a in tables])
    all_s = tree(jnp.add, [a[1:2] * jnp.exp2(a[0:1] - top_s) for a in tables])
    fades = [jnp.exp2(a[2:3] - top_u) for a in tables]
    all_u = tree(jnp.add, [a[3:4] * f for a, f in zip(tables, fades)])
    all_x = tree(jnp.add, [a[4:5] * f for a, f in zip(tables, fades)])
    lse_s = top_s + jnp.log2(all_s)
    lse_u = top_u + jnp.log2(all_u)
    loss = (lse_s - all_x / all_u) * LN2
    scale = jnp.log2(mine[5:6] * 10.0)
    for b in range(PAD // 128):
        cols = slice(b * 128, (b + 1) * 128)
        shift_s[cols, :] = jnp.transpose(jnp.broadcast_to((lse_s - scale)[:, cols], (128, 128)))
        shift_u[cols, :] = jnp.transpose(jnp.broadcast_to((lse_u - scale)[:, cols], (128, 128)))

    sheet = jnp.concatenate([loss[:, b * 128 : (b + 1) * 128] for b in range(PAD // 128)], axis=0)
    line = lax.broadcasted_iota(I32, (8, 128), 0)
    lane = lax.broadcasted_iota(I32, (8, 128), 1)
    sheet = jnp.where((line == 7) & (lane == 127), mine[6:7, 0:128], sheet)
    losses[z_low, z_high, x] = sheet
    lx_copies = [
        send(losses.at[z_low, z_high, x], losses.at[z_low, z_high, x], lx_ss.at[i], lx_rs.at[i], x_id(d))
        for i, d in enumerate((1, 2, 3))
    ]

    def block(q):
        return pl.ds(pl.multiple_of(q * 64, 64), 64)

    right, left, far = lax.rem(x + 1, NX), lax.rem(x + 3, NX), lax.rem(x + 2, NX)

    def halves(n):
        half = WIDTHS[n] // 2
        return pl.ds(0, half), pl.ds(half, half)

    relays, directs, sums = [], [], []
    nears, ends = [], []

    def send_x(n):
        low, high = halves(n)
        near = pl.ds(0, WIDTHS[n] // 2)
        relays.append([
            send(x_send.at[n, block(far), low], x_relay.at[n, 0, :, near], x_ss.at[n, 0], x_rs.at[n, 0], x_id(1)),
            send(x_send.at[n, block(far), high], x_relay.at[n, 1, :, near], x_ss.at[n, 1], x_rs.at[n, 1], x_id(-1)),
        ])
        directs.append([
            send(x_send.at[n, block(right), high], x_got.at[n, 0, :, high], x_ss.at[n, 2], x_rs.at[n, 2], x_id(1)),
            send(x_send.at[n, block(left), low], x_got.at[n, 1, :, low], x_ss.at[n, 3], x_rs.at[n, 3], x_id(-1)),
        ])

    def relay_x(n):
        low, high = halves(n)
        near = pl.ds(0, WIDTHS[n] // 2)
        out = []
        for i, (q, lanes, d) in enumerate(((right, low, 1), (left, high, -1))):
            relays[n][i].wait_recv()
            total = x_send[n, block(q), lanes].astype(F32) + x_relay[n, i, :, near].astype(F32)
            x_sum[n, i, :, near] = total.astype(BF16)
            out.append(send(x_sum.at[n, i, :, near], x_got.at[n, i, :, lanes], x_ss.at[n, 4 + i], x_rs.at[n, 4 + i], x_id(d)))
        sums.append(out)

    def send_z(n):
        for copy in directs[n] + sums[n]:
            copy.wait_recv()
        width = WIDTHS[n]
        size = width // 4
        total = own[n, :, :width] + x_got[n, 0, :, :width].astype(F32) + x_got[n, 1, :, :width].astype(F32)
        for q in range(NZ):
            piece = jnp.concatenate(
                [total[4 * q : 4 * q + 4, j * size : (j + 1) * size] for j in range(4)], axis=0
            )
            z_send[n, q % 4, q // 4, :, :size] = piece.astype(BF16)
        lanes = pl.ds(0, size)
        out = []
        for i, d in enumerate((1, -1)):
            group = lax.rem(z_low + d + 4, 4)
            out.append(send(z_send.at[n, group, :, :, lanes], z_near.at[n, i, :, :, lanes], z_ss.at[n, i], z_rs.at[n, i], z_id(d)))
        group = lax.rem(z_low + 2, 4)
        for i, d in enumerate((2, -2)):
            for k in range(2):
                spot = lax.rem(z + d * (1 + 2 * k) + NZ, NZ) // 4
                m = 2 + 2 * i + k
                out.append(send(z_send.at[n, group, spot, :, lanes], z_next.at[n, i, k, :, lanes], z_ss.at[n, m], z_rs.at[n, m], z_id(d)))
        nears.append(out)

    def relay_z(n):
        for copy in nears[n]:
            copy.wait_recv()
        lanes = pl.ds(0, WIDTHS[n] // 4)
        out = []
        for i, step in enumerate((1, 3, 2, 0)):
            k = lax.rem(z_high + step, 4)
            total = sum(
                (ref[..., lanes].astype(F32) for ref in (z_near.at[n, 0, k], z_near.at[n, 1, k])),
                z_send[n, z_low, k, :, lanes].astype(F32),
            )
            if step in (0, 1):
                total = total + z_next[n, 0, step, :, lanes].astype(F32)
            if step in (0, 3):
                total = total + z_next[n, 1, step // 3, :, lanes].astype(F32)
            if step == 0:
                z_own[n, :, lanes] = total
            else:
                z_sum[n, i, :, lanes] = total.astype(BF16)
                out.append(send(z_sum.at[n, i, :, lanes], z_got.at[n, i, :, lanes], z_ss.at[n, 6 + i], z_rs.at[n, 6 + i], z_id((4, -4, 8)[i])))
        ends.append(out)

    def finish(n):
        for copy in ends[n]:
            copy.wait_recv()
        size = WIDTHS[n] // 4
        total = z_own[n, :, :size]
        for i in range(3):
            total = total + z_got[n, i, :, :size].astype(F32)
        for j in range(4):
            at = STARTS[n] + j * size
            grad_out[:, at : at + size] = total[j * 4 : j * 4 + 4, :]

    def add_du(n, rows):
        add = lax.dot_general(
            grads[n % 2][rows, : WIDTHS[n]], protos[:, columns(n)], NT, preferred_element_type=F32
        )
        du[rows, :] = du[rows, :] + add if n else add

    for n in range(CHUNKS):
        shift = lane_parts(center[:, columns(n)] * K_U)

        def tile(t, carry, n=n, shift=shift):
            at = pl.multiple_of(t * TILE, TILE)
            if n:
                add_du(n - 1, pl.ds(at, TILE))
            for k in range(TILE // GROUP):
                there = pl.ds(pl.multiple_of(at + k * GROUP, GROUP), GROUP)
                less_s, less_u = shift_s[there, :], shift_u[there, :]
                s = lane_parts(dots[n][there, :])
                u = lane_parts(targets[n][there, :])
                for j in range(WIDTHS[n] // 128):
                    g = jnp.exp2(s[j] * K_S - less_s) - jnp.exp2(u[j] * K_U - (less_u + shift[j]))
                    grads[n % 2][there, j * 128 : (j + 1) * 128] = g.astype(BF16)
            return carry

        lax.fori_loop(0, TILES, tile, 0)
        if n:
            relay_x(n - 1)
        for j in range(WIDTHS[n] // 256):
            lanes = slice(j * 256, (j + 1) * 256)
            piece = jnp.dot(xt[...], grads[n % 2][:, lanes], preferred_element_type=F32)
            part[:, lanes] = piece
            x_send[n, :, lanes] = piece.astype(BF16)
        send_x(n)
        own[n, :, : WIDTHS[n]] = part[block(x), : WIDTHS[n]]
        if n == 0:
            for copy in lx_copies:
                copy.wait_recv()
            spot = losses.at[z_low, z_high]
            lz_copies = [
                send(spot, spot, lz_ss.at[i], lz_rs.at[i], z_id(d)) for i, d in enumerate((4, -4, 8))
            ]
        if n == 1:
            for copy in lz_copies:
                copy.wait_recv()
            spot = losses.at[z_low]
            ln_copies = [
                send(spot, spot, lz_ss.at[3 + i], lz_rs.at[3 + i], z_id(d)) for i, d in enumerate((1, -1, 2))
            ]
        if n == CHUNKS - 1:
            for t in range(TILES):
                add_du(n, pl.ds(t * TILE, TILE))
            for q in range(NY * NC):
                size = min(128, CAP - q * 128)
                f_send[q % NC, q // NC, :size, :] = du[q * 128 : q * 128 + size, :].astype(BF16)
                if size < 128:
                    f_send[q % NC, q // NC, size:, :] = jnp.zeros((128 - size, D), BF16)
            pair_copy = send(f_send.at[1 - c], f_pair, f_ss.at[0], f_rs.at[0], pair)
        if n >= 2:
            send_z(n - 2)
        if n >= 3:
            relay_z(n - 3)
    send_z(CHUNKS - 2)

    pair_copy.wait_recv()
    f_sum[...] = (f_send[c].astype(F32) + f_pair[...].astype(F32)).astype(BF16)
    f_copies = [
        send(f_sum.at[lax.rem(y + d, NY)], f_got.at[d - 1], f_ss.at[d], f_rs.at[d], y_id(d))
        for d in range(1, NY)
    ]
    relay_x(CHUNKS - 1)
    relay_z(CHUNKS - 3)
    for copy in f_copies:
        copy.wait_recv()
    total = f_sum[y].astype(F32)
    for i in range(NY - 1):
        total = total + f_got[i].astype(F32)
    rows = rows_in[pl.ds(pl.multiple_of(pro * 128, 128), 128), :].astype(F32)
    length = jnp.sqrt(jnp.sum(rows * rows, axis=1, keepdims=True) + 1e-6)
    unit = rows / length
    total = (total - unit * jnp.sum(unit * total, axis=1, keepdims=True)) / length
    f_all[c, y] = total.astype(BF16)
    g_copies = [
        send(f_all.at[c, y], f_all.at[c, y], f_ss.at[3 + d], f_rs.at[3 + d], y_id(d)) for d in range(1, NY)
    ]

    send_z(CHUNKS - 1)
    relay_z(CHUNKS - 2)
    for copy in g_copies:
        copy.wait_recv()
    share = send(f_all.at[c], f_all.at[c], f_ss.at[7], f_rs.at[7], pair)
    for n in range(CHUNKS - 2):
        finish(n)
    for copy in ln_copies:
        copy.wait_recv()
    for q in range(NZ):
        loss_out[q * NX : (q + 1) * NX] = losses[q % 4, q // 4]
    relay_z(CHUNKS - 1)
    finish(CHUNKS - 2)
    share.wait_recv()
    for q in range(NY * NC):
        feat_out[q * 128 : (q + 1) * 128, :] = f_all[q % NC, q // NC]
    finish(CHUNKS - 1)
    for copy in stat_copies + lx_copies + lz_copies + ln_copies + f_copies + g_copies + [pair_copy, share]:
        copy.wait_send()
    for n in range(CHUNKS):
        for copy in relays[n] + directs[n] + sums[n] + nears[n] + ends[n]:
            copy.wait_send()


def place_kernel(rank, feat, losses, perm, token_out, loss_out):
    turned = jnp.transpose(jnp.concatenate([rank[...], jnp.zeros((112, 128), F32)], axis=0))
    spot = lax.broadcasted_iota(I32, (128, PAD), 1).astype(F32)
    for b in range(13):
        size = min(128, SEQ - b * 128)
        pick = jnp.where(turned[:size, b : b + 1] == spot[:size], 1.0, 0.0).astype(BF16)
        token_out[b * 128 : b * 128 + size, :] = jnp.dot(
            pick, feat[...], preferred_element_type=F32
        ).astype(BF16)

    me = lax.axis_index("tok")
    table = losses[...]
    lane2 = lax.broadcasted_iota(I32, (TOK, 128), 1)
    counts = jnp.sum(jnp.where(lane2 == 127, table[:, 7, :], 0.0), axis=1, keepdims=True)
    counts = jnp.broadcast_to(counts, (TOK, 128))
    r_i = lax.broadcasted_iota(I32, (TOK, TOK), 0)
    c_i = lax.broadcasted_iota(I32, (TOK, TOK), 1)
    offsets = jnp.dot(
        jnp.where(c_i < r_i, 1.0, 0.0), counts, preferred_element_type=F32, precision=lax.Precision.HIGHEST
    )
    offsets = jnp.round(offsets).astype(I32)
    sizes = counts.astype(I32)
    slots = lax.broadcasted_iota(I32, (1, TOK), 1)
    slot = jnp.sum(jnp.where(perm[...] == me, slots, 0), axis=1, keepdims=True)
    first = (slot - offsets) & 63
    shape = (TOK, 8, 128)
    first3 = jnp.broadcast_to(first[:, None, :], shape)
    off3 = jnp.broadcast_to(offsets[:, None, :], shape)
    size3 = jnp.broadcast_to(sizes[:, None, :], shape)
    lane3 = lax.broadcasted_iota(I32, shape, 2)
    index3 = lax.broadcasted_iota(I32, shape, 1) * 128 + first3
    places = lax.broadcasted_iota(I32, (TOK * 8, 128), 1)
    for q in range(OUT // 128):
        acc = jnp.zeros((1, 128), F32)
        for part in range(2):
            index = index3 + part * 64
            value = jnp.sum(
                jnp.where((lane3 == first3 + part * 64) & (index < size3), table, 0.0), axis=2, keepdims=True
            )
            value = jnp.broadcast_to(value, shape).reshape(TOK * 8, 128)
            goal = ((off3 + index) >> 6).reshape(TOK * 8, 128)
            acc = acc + jnp.sum(jnp.where(goal == places + q * 128, value, 0.0), axis=0, keepdims=True)
        loss_out[:, q * 128 : (q + 1) * 128] = acc


def vmem(count):
    return [pl.BlockSpec(memory_space=pltpu.VMEM)] * count


def on_device(student, teacher, mask, perm, cot, protos, center):
    shape = jax.ShapeDtypeStruct
    hbm = pl.BlockSpec(memory_space=pltpu.HBM)
    ram = pltpu.VMEM
    dma = lambda *s: pltpu.SemaphoreType.DMA(s)
    peers = NY * NC - 1
    grad, feat, losses, rank = pl.pallas_call(
        main_kernel,
        out_shape=(
            shape((4, LOCAL), F32), shape((PAD, D), BF16), shape((TOK, 8, 128), F32), shape((16, 128), F32),
        ),
        in_specs=[hbm] * 3 + vmem(1) + [hbm] * 2,
        out_specs=tuple(vmem(4)),
        scratch_shapes=[
            ram((SEQ, D), BF16), ram((SEQ, D), BF16), ram((1, SEQ), I32), ram((D, LOCAL), BF16), ram((1, LOCAL), F32),
            dma(5), ram((1, 13 * 128), F32),
            ram((PAD, D), BF16), ram((CAP, D), BF16), ram((CAP, D), BF16), ram((D, PAD), BF16),
        ]
        + [ram((CAP, w), F32) for w in WIDTHS] * 2
        + [ram((PAD, 128), F32)]
        + [ram((CAP, 128), F32)] * 4
        + [
            ram((8, PAD), F32), ram((peers, 8, PAD), F32), ram((PAD, 128), F32), ram((PAD, 128), F32),
            ram((PAD, LANES), BF16), ram((PAD, LANES), BF16),
            ram((CAP, D), F32), ram((D, LANES), F32), ram((CHUNKS, 64, LANES), F32),
            ram((CHUNKS, D, LANES), BF16),
            ram((CHUNKS, 2, 64, LANES // 2), BF16), ram((CHUNKS, 2, 64, LANES // 2), BF16),
            ram((CHUNKS, 2, 64, LANES), BF16),
            ram((CHUNKS, 4, 4, 16, 256), BF16), ram((CHUNKS, 2, 4, 16, 256), BF16), ram((CHUNKS, 2, 2, 16, 256), BF16),
            ram((CHUNKS, 3, 16, 256), BF16), ram((CHUNKS, 16, 256), F32), ram((CHUNKS, 3, 16, 256), BF16),
            ram((NC, NY, 128, D), BF16), ram((NY, 128, D), BF16), ram((NY, 128, D), BF16),
            ram((NY - 1, 128, D), BF16), ram((NC, NY, 128, D), BF16),
            ram((4, 4, NX, 8, 128), F32),
            dma(peers), dma(peers),
            dma(3), dma(3),
            dma(6), dma(6),
            dma(CHUNKS, 6), dma(CHUNKS, 6),
            dma(CHUNKS, 9), dma(CHUNKS, 9),
            dma(8), dma(8),
        ],
        compiler_params=pltpu.CompilerParams(
            collective_id=1, has_side_effects=True, vmem_limit_bytes=60 << 20
        ),
        name="main",
    )(student[0], teacher[0], mask, cot.reshape(1, 1), protos, center.reshape(1, LOCAL))

    tokens, row_loss = pl.pallas_call(
        place_kernel,
        out_shape=(shape((SEQ, D), BF16), shape((1, OUT), F32)),
        in_specs=vmem(4),
        out_specs=tuple(vmem(2)),
        compiler_params=pltpu.CompilerParams(vmem_limit_bytes=48 << 20),
        name="place",
    )(rank, feat, losses, perm.reshape(1, TOK))
    return tokens[None], grad, row_loss.reshape(OUT)


def solution(mesh):
    in_specs = (
        P("tok", None, None),
        P("tok", None, None),
        P("tok", None),
        P(),
        P("tok"),
        P(None, "proto"),
        P("proto"),
    )
    out_specs = (P("tok", None, None), P("tok", "proto"), P("tok"))
    return jax.shard_map(
        on_device, mesh=mesh, in_specs=in_specs, out_specs=out_specs, check_vma=False
    )
```

time: 93.5 us -> 89.1 us (0.953)
  the two profiles are of different devices: /device:TPU:1 before, /device:TPU:2 now
where the time goes in v2:
time: 89.1 us; the launch traced here: 88.8 us
  Pallas kernels  83.3 us (93%)
  local copies, waits for them, and re-layouts  4.16 us (5%)
  between operations  1.33 us (1%)
    pallas_call x1, Pallas kernels, on_device(): pl.pallas_call(main_kernel, out_shape=(shape((4, LOCAL), F32), shape((PAD...  81 us
    unnamed x9, local copies, waits for them, and re-layouts  4.16 us
    pallas_call x1, Pallas kernels, on_device(): pl.pallas_call(place_kernel, out_shape=(shape((SEQ, D), BF16), shape((1,...  2.32 us

profile of v2, /device:TPU:2, one launch (start us, length us, event | category | flops | bytes accessed | tf_op | source)
XLA Modules:
  0.0 88.8 jit_solution(1024946099959262301)
XLA Ops:
  0.6 0.0 copy-start.3
  1.3 81.0 %main.1 = (f32[4,4096]{1,0:T(4,128)}, bf16[1024,256]{1,0:T(8,128)(2,1)}, f32[64,8,128]{2,1,0:T(8,128)}, f32[16,128]{1,0:T(8,128)}) custom-call(bf16[1568,256]{1,0:T(8,128)(2,1)} %bitcast.9, bf16[1568,256]{1,0:T(8,128)(2,1)} %bitcast.10, s32[1,1568]{1,0:T(1,128)} %mask_in.1, f32[1,1]{1,0:T(1,128)} %bitcast.7.cot, bf16[256,4096]{1,0:T(8,128)(2,1)} %protos_in.1, ...), custom_call_target="tpu_custom_call" | custom-call | tf_op jit(solution)/shard_map/main/pallas_call | solution.py:514
  82.3 0.0 copy-done.3
  82.3 0.0 copy-start
  82.3 1.0 %copy-done = bf16[1024,256]{1,0:T(8,128)(2,1)S(1)} copy-done((bf16[1024,256]{1,0:T(8,128)(2,1)S(1)}, bf16[1024,256]{1,0:T(8,128)(2,1)}, u32[]{:S(2)}) %copy-start) | copy-done | bytes 524312
  83.4 0.0 copy-start.1
  83.4 0.9 %copy-done.1 = f32[64,8,128]{2,1,0:T(8,128)S(1)} copy-done((f32[64,8,128]{2,1,0:T(8,128)S(1)}, f32[64,8,128]{2,1,0:T(8,128)}, u32[]{:S(2)}) %copy-start.1) | copy-done | bytes 262168
  84.3 0.0 copy-start.2
  84.3 0.7 copy-done.2
  85.0 2.3 %place.1 = (bf16[1568,256]{1,0:T(8,128)(2,1)}, f32[1,512]{1,0:T(1,128)}) custom-call(f32[16,128]{1,0:T(8,128)S(1)} %copy-done.2, bf16[1024,256]{1,0:T(8,128)(2,1)S(1)} %copy-done, f32[64,8,128]{2,1,0:T(8,128)S(1)} %copy-done.1, s32[1,64]{1,0:T(1,128)S(1)} %bitcast.8), custom_call_target="tpu_custom_call" | custom-call | tf_op jit(solution)/shard_map/place/pallas_call | solution.py:554
  87.3 1.5 %copy.12 = f32[4,4096]{1,0:T(4,128)} copy(f32[4,4096]{1,0:T(4,128)} %get-tuple-element.19) | data formatting | bytes 131072
Async XLA Ops:
  0.6 81.7 %copy-start.3 = (s32[64]{0:T(128)S(1)}, s32[64]{0:T(128)}, u32[]{:S(2)}) copy-start(s32[64]{0:T(128)} %param.10) | copy-start | bytes 772
  82.3 1.0 %copy-start = (bf16[1024,256]{1,0:T(8,128)(2,1)S(1)}, bf16[1024,256]{1,0:T(8,128)(2,1)}, u32[]{:S(2)}) copy-start(bf16[1024,256]{1,0:T(8,128)(2,1)} %get-tuple-element.10.feat) | copy-start | bytes 1572868
  83.4 0.9 %copy-start.1 = (f32[64,8,128]{2,1,0:T(8,128)S(1)}, f32[64,8,128]{2,1,0:T(8,128)}, u32[]{:S(2)}) copy-start(f32[64,8,128]{2,1,0:T(8,128)} %get-tuple-element.11.losses) | copy-start | bytes 786436
  84.3 0.7 copy-start.2

commit v3 on v2

--- a/solution.py
+++ b/solution.py
@@ -22,6 +22,8 @@
 TILE = 480
 TILES = CAP // TILE
 GROUP = 16
+STEP = 64
+ROWS = ((0, 512), (512, CAP - 512))
 OUT = 512
 
 LOG2E = 1.4426950408889634
@@ -42,13 +44,60 @@
     return parts[0]
 
 
+def place_tokens(rank, feat, token_out):
+    turned = jnp.transpose(jnp.concatenate([rank[...], jnp.zeros((112, 128), F32)], axis=0))
+    spot = lax.broadcasted_iota(I32, (128, PAD), 1).astype(F32)
+    for b in range(13):
+        size = min(128, SEQ - b * 128)
+        pick = jnp.where(turned[:size, b : b + 1] == spot[:size], 1.0, 0.0).astype(BF16)
+        token_out[b * 128 : b * 128 + size, :] = jnp.dot(
+            pick, feat[...], preferred_element_type=F32
+        ).astype(BF16)
+
+
+def place_losses(table, perm, me):
+    results = []
+    lane2 = lax.broadcasted_iota(I32, (TOK, 128), 1)
+    counts = jnp.sum(jnp.where(lane2 == 127, table[:, 7, :], 0.0), axis=1, keepdims=True)
+    counts = jnp.broadcast_to(counts, (TOK, 128))
+    r_i = lax.broadcasted_iota(I32, (TOK, TOK), 0)
+    c_i = lax.broadcasted_iota(I32, (TOK, TOK), 1)
+    offsets = jnp.dot(
+        jnp.where(c_i < r_i, 1.0, 0.0), counts, preferred_element_type=F32, precision=lax.Precision.HIGHEST
+    )
+    offsets = jnp.round(offsets).astype(I32)
+    sizes = counts.astype(I32)
+    slots = lax.broadcasted_iota(I32, (1, TOK), 1)
+    slot = jnp.sum(jnp.where(perm == me, slots, 0), axis=1, keepdims=True)
+    first = (slot - offsets) & 63
+    shape = (TOK, 8, 128)
+    first3 = jnp.broadcast_to(first[:, None, :], shape)
+    off3 = jnp.broadcast_to(offsets[:, None, :], shape)
+    size3 = jnp.broadcast_to(sizes[:, None, :], shape)
+    lane3 = lax.broadcasted_iota(I32, shape, 2)
+    index3 = lax.broadcasted_iota(I32, shape, 1) * 128 + first3
+    places = lax.broadcasted_iota(I32, (TOK * 8, 128), 1)
+    for q in range(OUT // 128):
+        acc = jnp.zeros((1, 128), F32)
+        for part in range(2):
+            index = index3 + part * 64
+            value = jnp.sum(
+                jnp.where((lane3 == first3 + part * 64) & (index < size3), table, 0.0), axis=2, keepdims=True
+            )
+            value = jnp.broadcast_to(value, shape).reshape(TOK * 8, 128)
+            goal = ((off3 + index) >> 6).reshape(TOK * 8, 128)
+            acc = acc + jnp.sum(jnp.where(goal == places + q * 128, value, 0.0), axis=0, keepdims=True)
+        results.append(acc)
+    return jnp.concatenate(results, axis=1)
+
+
 def main_kernel(
-    student_in, teacher_in, mask_in, cot, protos_in, center_in,
-    grad_out, feat_out, loss_out, rank_out,
-    student, teacher, mask, protos, center, in_sem, rank_row, rows_in, xh, yh, xt,
+    student_in, teacher_in, mask_in, cot, protos_in, center_in, perm,
+    token_out, grad_out, loss_out,
+    student, teacher, mask, protos, center, in_sem, out_sem, rank_out, rank_row, rows_in, xh, yh, xt,
     dots_a, dots_b, dots_c, dots_d, dots_e, targets_a, targets_b, targets_c, targets_d, targets_e,
     peak_s, sum_s, peak_u, sum_u, cross, stats,
-    stat_got, shift_s, shift_u, grads_a, grads_b, du, part, own,
+    stat_got, grads, du, part, own,
     x_send, x_relay, x_sum, x_got, z_send, z_near, z_next, z_sum, z_own, z_got,
     f_send, f_pair, f_sum, f_got, f_all, losses,
     stat_ss, stat_rs, lx_ss, lx_rs, lz_ss, lz_rs, x_ss, x_rs, z_ss, z_rs, f_ss, f_rs,
@@ -66,7 +115,8 @@
         copy.start()
     dots = (dots_a, dots_b, dots_c, dots_d, dots_e)
     targets = (targets_a, targets_b, targets_c, targets_d, targets_e)
-    grads = (grads_a, grads_b)
+    shift_s, shift_u = sum_s, sum_u
+    feat = teacher.at[pl.ds(0, PAD)]
 
     tok = lax.axis_index("tok")
     pro = lax.axis_index("proto")
@@ -150,51 +200,46 @@
         dots[n][rows, :] = jnp.dot(xh[rows, :], protos[:, columns(n)], preferred_element_type=F32)
         targets[n][rows, :] = jnp.dot(yh[rows, :], protos[:, columns(n)], preferred_element_type=F32)
 
-    def first(t, carry):
-        scores(0, pl.ds(pl.multiple_of(t * TILE, TILE), TILE))
-        return carry
-
-    lax.fori_loop(0, TILES, first, 0)
-    for n in range(CHUNKS):
-        shift = lane_parts(center[:, columns(n)] * K_U)
-
-        def gather(t, carry, n=n, shift=shift):
-            at = pl.multiple_of(t * TILE, TILE)
-            if n + 1 < CHUNKS:
-                scores(n + 1, pl.ds(at, TILE))
-            for k in range(TILE // GROUP):
-                there = pl.ds(pl.multiple_of(at + k * GROUP, GROUP), GROUP)
-                s = lane_parts(dots[n][there, :] * K_S)
-                u = [a * K_U - b for a, b in zip(lane_parts(targets[n][there, :]), shift)]
-                top_s = tree(jnp.maximum, s)
-                top_u = tree(jnp.maximum, u)
-                if n:
-                    old_s, old_u = peak_s[there, :], peak_u[there, :]
-                    top_s = jnp.maximum(top_s, old_s)
-                    top_u = jnp.maximum(top_u, old_u)
-                add_s = tree(jnp.add, [jnp.exp2(a - top_s) for a in s])
-                tilted = [jnp.exp2(a - top_u) for a in u]
-                add_u = tree(jnp.add, tilted)
-                add_x = tree(jnp.add, [a * b for a, b in zip(tilted, s)])
-                if n:
-                    fade_u = jnp.exp2(old_u - top_u)
-                    add_s = add_s + sum_s[there, :] * jnp.exp2(old_s - top_s)
-                    add_u = add_u + sum_u[there, :] * fade_u
-                    add_x = add_x + cross[there, :] * fade_u
-                peak_s[there, :] = top_s
-                peak_u[there, :] = top_u
-                sum_s[there, :] = add_s
-                sum_u[there, :] = add_u
-                cross[there, :] = add_x
-            return carry
-
-        lax.fori_loop(0, TILES, gather, 0)
-
     weight = cot[...] / count
-    lane = lax.broadcasted_iota(I32, (TILE, 128), 1)
-
-    def merge(t, carry):
-        at = pl.ds(pl.multiple_of(t * TILE, TILE), TILE)
+    line8 = lax.broadcasted_iota(I32, (8, 128), 0)
+    peak_s[CAP:, :] = jnp.ones((PAD - CAP, 128), F32)
+
+    def forward(r):
+        start, size = ROWS[r]
+        for n in range(CHUNKS):
+            scores(n, pl.ds(start, size))
+            shift = lane_parts(center[:, columns(n)] * K_U)
+
+            def gather(t, carry, n=n, shift=shift):
+                for k in range(STEP // GROUP):
+                    there = pl.ds(pl.multiple_of(start + t * STEP + k * GROUP, GROUP), GROUP)
+                    s = lane_parts(dots[n][there, :] * K_S)
+                    u = [a * K_U - b for a, b in zip(lane_parts(targets[n][there, :]), shift)]
+                    top_s = tree(jnp.maximum, s)
+                    top_u = tree(jnp.maximum, u)
+                    if n:
+                        old_s, old_u = peak_s[there, :], peak_u[there, :]
+                        top_s = jnp.maximum(top_s, old_s)
+                        top_u = jnp.maximum(top_u, old_u)
+                    add_s = tree(jnp.add, [jnp.exp2(a - top_s) for a in s])
+                    tilted = [jnp.exp2(a - top_u) for a in u]
+                    add_u = tree(jnp.add, tilted)
+                    add_x = tree(jnp.add, [a * b for a, b in zip(tilted, s)])
+                    if n:
+                        fade_u = jnp.exp2(old_u - top_u)
+                        add_s = add_s + sum_s[there, :] * jnp.exp2(old_s - top_s)
+                        add_u = add_u + sum_u[there, :] * fade_u
+                        add_x = add_x + cross[there, :] * fade_u
+                    peak_s[there, :] = top_s
+                    peak_u[there, :] = top_u
+                    sum_s[there, :] = add_s
+                    sum_u[there, :] = add_u
+                    cross[there, :] = add_x
+                return carry
+
+            lax.fori_loop(0, size // STEP, gather, 0)
+        at = slice(start, start + size)
+        lane = lax.broadcasted_iota(I32, (size, 128), 1)
         top_s = jnp.max(peak_s[at, :], axis=1, keepdims=True)
         top_u = jnp.max(peak_u[at, :], axis=1, keepdims=True)
         fade_u = jnp.exp2(peak_u[at, :] - top_u)
@@ -203,17 +248,10 @@
         all_x = jnp.sum(cross[at, :] * fade_u, axis=1, keepdims=True)
         packed = jnp.where(lane == 0, top_s, jnp.where(lane == 1, all_s, jnp.where(lane == 2, top_u, jnp.where(lane == 3, all_u, all_x))))
         peak_s[at, :] = packed
-        return carry
-
-    lax.fori_loop(0, TILES, merge, 0)
-    peak_s[CAP:, :] = jnp.ones((PAD - CAP, 128), F32)
-    line8 = lax.broadcasted_iota(I32, (8, 128), 0)
-    for b in range(PAD // 128):
-        turned = jnp.transpose(peak_s[b * 128 : (b + 1) * 128, :])[0:8, :]
-        turned = jnp.where(line8 == 5, weight, jnp.where(line8 == 6, count, turned))
-        stats[:, b * 128 : (b + 1) * 128] = turned
-
-    pl.semaphore_wait(barrier, len(everyone))
+        for b in range(4):
+            turned = jnp.transpose(peak_s[start + b * 128 : start + (b + 1) * 128, :])[0:8, :]
+            turned = jnp.where(line8 == 5, weight, jnp.where(line8 == 6, count, turned))
+            stats[r, :, b * 128 : (b + 1) * 128] = turned
 
     def send(src, dst, ss, rs, device):
         copy = pltpu.make_async_remote_copy(
@@ -222,34 +260,75 @@
         copy.start()
         return copy
 
-    stat_copies = [
-        send(stats, stat_got.at[i], stat_ss.at[i], stat_rs.at[i], q) for i, q in enumerate(p_ids)
-    ]
-    for ref in grads:
-        ref[CAP:, :] = jnp.zeros((PAD - CAP, LANES), BF16)
-    for copy in stat_copies:
-        copy.wait_recv()
-    mine = stats[...]
-    tables = [mine] + [stat_got[i] for i in range(NY * NC - 1)]
-    top_s = tree(jnp.maximum, [a[0:1] for a in tables])
-    top_u = tree(jnp.maximum, [a[2:3] for a in tables])
-    all_s = tree(jnp.add, [a[1:2] * jnp.exp2(a[0:1] - top_s) for a in tables])
-    fades = [jnp.exp2(a[2:3] - top_u) for a in tables]
-    all_u = tree(jnp.add, [a[3:4] * f for a, f in zip(tables, fades)])
-    all_x = tree(jnp.add, [a[4:5] * f for a, f in zip(tables, fades)])
-    lse_s = top_s + jnp.log2(all_s)
-    lse_u = top_u + jnp.log2(all_u)
-    loss = (lse_s - all_x / all_u) * LN2
-    scale = jnp.log2(mine[5:6] * 10.0)
-    for b in range(PAD // 128):
-        cols = slice(b * 128, (b + 1) * 128)
-        shift_s[cols, :] = jnp.transpose(jnp.broadcast_to((lse_s - scale)[:, cols], (128, 128)))
-        shift_u[cols, :] = jnp.transpose(jnp.broadcast_to((lse_u - scale)[:, cols], (128, 128)))
+    stat_copies = []
+
+    def share_stats(r):
+        stat_copies.append(
+            [
+                send(stats.at[r], stat_got.at[i, r], stat_ss.at[i, r], stat_rs.at[i, r], q)
+                for i, q in enumerate(p_ids)
+            ]
+        )
+
+    def join_stats(r):
+        for copy in stat_copies[r]:
+            copy.wait_recv()
+        mine = stats[r]
+        tables = [mine] + [stat_got[i, r] for i in range(NY * NC - 1)]
+        top_s = tree(jnp.maximum, [a[0:1] for a in tables])
+        top_u = tree(jnp.maximum, [a[2:3] for a in tables])
+        all_s = tree(jnp.add, [a[1:2] * jnp.exp2(a[0:1] - top_s) for a in tables])
+        fades = [jnp.exp2(a[2:3] - top_u) for a in tables]
+        all_u = tree(jnp.add, [a[3:4] * f for a, f in zip(tables, fades)])
+        all_x = tree(jnp.add, [a[4:5] * f for a, f in zip(tables, fades)])
+        lse_s = top_s + jnp.log2(all_s)
+        lse_u = top_u + jnp.log2(all_u)
+        scale = jnp.log2(mine[5:6] * 10.0)
+        for b in range(4):
+            cols = slice(b * 128, (b + 1) * 128)
+            rows = slice(r * 512 + b * 128, r * 512 + (b + 1) * 128)
+            shift_s[rows, :] = jnp.transpose(jnp.broadcast_to((lse_s - scale)[:, cols], (128, 128)))
+            shift_u[rows, :] = jnp.transpose(jnp.broadcast_to((lse_u - scale)[:, cols], (128, 128)))
+        return (lse_s - all_x / all_u) * LN2
+
+    def gradients(n, r):
+        start, size = ROWS[r]
+        shift = lane_parts(center[:, columns(n)] * K_U)
+
+        def tile(t, carry):
+            for k in range(STEP // GROUP):
+                there = pl.ds(pl.multiple_of(start + t * STEP + k * GROUP, GROUP), GROUP)
+                less_s, less_u = shift_s[there, :], shift_u[there, :]
+                s = lane_parts(dots[n][there, :])
+                u = lane_parts(targets[n][there, :])
+                for j in range(WIDTHS[n] // 128):
+                    g = jnp.exp2(s[j] * K_S - less_s) - jnp.exp2(u[j] * K_U - (less_u + shift[j]))
+                    at = STARTS[n] + j * 128
+                    grads[there, at : at + 128] = g.astype(BF16)
+            return carry
+
+        lax.fori_loop(0, size // STEP, tile, 0)
+
+    def gradient_rows(r):
+        at = slice(ROWS[r][0], ROWS[r][0] + ROWS[r][1])
+        du[at, :] = lax.dot_general(grads[at, :], protos[...], NT, preferred_element_type=F32)
+
+    forward(0)
+    pl.semaphore_wait(barrier, len(everyone))
+    share_stats(0)
+    forward(1)
+    share_stats(1)
+    grads[CAP:, :] = jnp.zeros((PAD - CAP, LOCAL), BF16)
+    loss_a = join_stats(0)
+    for n in range(CHUNKS):
+        gradients(n, 0)
+    loss_b = join_stats(1)
+    loss = jnp.concatenate([loss_a, loss_b], axis=1)
 
     sheet = jnp.concatenate([loss[:, b * 128 : (b + 1) * 128] for b in range(PAD // 128)], axis=0)
     line = lax.broadcasted_iota(I32, (8, 128), 0)
     lane = lax.broadcasted_iota(I32, (8, 128), 1)
-    sheet = jnp.where((line == 7) & (lane == 127), mine[6:7, 0:128], sheet)
+    sheet = jnp.where((line == 7) & (lane == 127), stats[0, 6:7, 0:128], sheet)
     losses[z_low, z_high, x] = sheet
     lx_copies = [
         send(losses.at[z_low, z_high, x], losses.at[z_low, z_high, x], lx_ss.at[i], lx_rs.at[i], x_id(d))
@@ -348,39 +427,18 @@
             at = STARTS[n] + j * size
             grad_out[:, at : at + size] = total[j * 4 : j * 4 + 4, :]
 
-    def add_du(n, rows):
-        add = lax.dot_general(
-            grads[n % 2][rows, : WIDTHS[n]], protos[:, columns(n)], NT, preferred_element_type=F32
-        )
-        du[rows, :] = du[rows, :] + add if n else add
-
     for n in range(CHUNKS):
-        shift = lane_parts(center[:, columns(n)] * K_U)
-
-        def tile(t, carry, n=n, shift=shift):
-            at = pl.multiple_of(t * TILE, TILE)
-            if n:
-                add_du(n - 1, pl.ds(at, TILE))
-            for k in range(TILE // GROUP):
-                there = pl.ds(pl.multiple_of(at + k * GROUP, GROUP), GROUP)
-                less_s, less_u = shift_s[there, :], shift_u[there, :]
-                s = lane_parts(dots[n][there, :])
-                u = lane_parts(targets[n][there, :])
-                for j in range(WIDTHS[n] // 128):
-                    g = jnp.exp2(s[j] * K_S - less_s) - jnp.exp2(u[j] * K_U - (less_u + shift[j]))
-                    grads[n % 2][there, j * 128 : (j + 1) * 128] = g.astype(BF16)
-            return carry
-
-        lax.fori_loop(0, TILES, tile, 0)
-        if n:
-            relay_x(n - 1)
+        gradients(n, 1)
         for j in range(WIDTHS[n] // 256):
             lanes = slice(j * 256, (j + 1) * 256)
-            piece = jnp.dot(xt[...], grads[n % 2][:, lanes], preferred_element_type=F32)
+            at = STARTS[n] + j * 256
+            piece = jnp.dot(xt[...], grads[:, at : at + 256], preferred_element_type=F32)
             part[:, lanes] = piece
             x_send[n, :, lanes] = piece.astype(BF16)
         send_x(n)
         own[n, :, : WIDTHS[n]] = part[block(x), : WIDTHS[n]]
+        if n:
+            relay_x(n - 1)
         if n == 0:
             for copy in lx_copies:
                 copy.wait_recv()
@@ -389,6 +447,7 @@
                 send(spot, spot, lz_ss.at[i], lz_rs.at[i], z_id(d)) for i, d in enumerate((4, -4, 8))
             ]
         if n == 1:
+            gradient_rows(0)
             for copy in lz_copies:
                 copy.wait_recv()
             spot = losses.at[z_low]
@@ -396,8 +455,7 @@
                 send(spot, spot, lz_ss.at[3 + i], lz_rs.at[3 + i], z_id(d)) for i, d in enumerate((1, -1, 2))
             ]
         if n == CHUNKS - 1:
-            for t in range(TILES):
-                add_du(n, pl.ds(t * TILE, TILE))
+            gradient_rows(1)
             for q in range(NY * NC):
                 size = min(128, CAP - q * 128)
                 f_send[q % NC, q // NC, :size, :] = du[q * 128 : q * 128 + size, :].astype(BF16)
@@ -441,64 +499,23 @@
         finish(n)
     for copy in ln_copies:
         copy.wait_recv()
-    for q in range(NZ):
-        loss_out[q * NX : (q + 1) * NX] = losses[q % 4, q // 4]
+    table = jnp.concatenate([losses[q % 4, q // 4] for q in range(NZ)], axis=0)
+    loss_out[...] = place_losses(table, perm[...], tok)
     relay_z(CHUNKS - 1)
     finish(CHUNKS - 2)
     share.wait_recv()
     for q in range(NY * NC):
-        feat_out[q * 128 : (q + 1) * 128, :] = f_all[q % NC, q // NC]
+        feat[q * 128 : (q + 1) * 128, :] = f_all[q % NC, q // NC]
+    place_tokens(rank_out, feat, student)
+    result = pltpu.make_async_copy(student, token_out, out_sem.at[0])
+    result.start()
     finish(CHUNKS - 1)
-    for copy in stat_copies + lx_copies + lz_copies + ln_copies + f_copies + g_copies + [pair_copy, share]:
+    result.wait()
+    for copy in stat_copies[0] + stat_copies[1] + lx_copies + lz_copies + ln_copies + f_copies + g_copies + [pair_copy, share]:
         copy.wait_send()
     for n in range(CHUNKS):
         for copy in relays[n] + directs[n] + sums[n] + nears[n] + ends[n]:
             copy.wait_send()
-
-
-def place_kernel(rank, feat, losses, perm, token_out, loss_out):
-    turned = jnp.transpose(jnp.concatenate([rank[...], jnp.zeros((112, 128), F32)], axis=0))
-    spot = lax.broadcasted_iota(I32, (128, PAD), 1).astype(F32)
-    for b in range(13):
-        size = min(128, SEQ - b * 128)
-        pick = jnp.where(turned[:size, b : b + 1] == spot[:size], 1.0, 0.0).astype(BF16)
-        token_out[b * 128 : b * 128 + size, :] = jnp.dot(
-            pick, feat[...], preferred_element_type=F32
-        ).astype(BF16)
-
-    me = lax.axis_index("tok")
-    table = losses[...]
-    lane2 = lax.broadcasted_iota(I32, (TOK, 128), 1)
-    counts = jnp.sum(jnp.where(lane2 == 127, table[:, 7, :], 0.0), axis=1, keepdims=True)
-    counts = jnp.broadcast_to(counts, (TOK, 128))
-    r_i = lax.broadcasted_iota(I32, (TOK, TOK), 0)
-    c_i = lax.broadcasted_iota(I32, (TOK, TOK), 1)
-    offsets = jnp.dot(
-        jnp.where(c_i < r_i, 1.0, 0.0), counts, preferred_element_type=F32, precision=lax.Precision.HIGHEST
-    )
-    offsets = jnp.round(offsets).astype(I32)
-    sizes = counts.astype(I32)
-    slots = lax.broadcasted_iota(I32, (1, TOK), 1)
-    slot = jnp.sum(jnp.where(perm[...] == me, slots, 0), axis=1, keepdims=True)
-    first = (slot - offsets) & 63
-    shape = (TOK, 8, 128)
-    first3 = jnp.broadcast_to(first[:, None, :], shape)
-    off3 = jnp.broadcast_to(offsets[:, None, :], shape)
-    size3 = jnp.broadcast_to(sizes[:, None, :], shape)
-    lane3 = lax.broadcasted_iota(I32, shape, 2)
-    index3 = lax.broadcasted_iota(I32, shape, 1) * 128 + first3
-    places = lax.broadcasted_iota(I32, (TOK * 8, 128), 1)
-    for q in range(OUT // 128):
-        acc = jnp.zeros((1, 128), F32)
-        for part in range(2):
-            index = index3 + part * 64
-            value = jnp.sum(
-                jnp.where((lane3 == first3 + part * 64) & (index < size3), table, 0.0), axis=2, keepdims=True
-            )
-            value = jnp.broadcast_to(value, shape).reshape(TOK * 8, 128)
-            goal = ((off3 + index) >> 6).reshape(TOK * 8, 128)
-            acc = acc + jnp.sum(jnp.where(goal == places + q * 128, value, 0.0), axis=0, keepdims=True)
-        loss_out[:, q * 128 : (q + 1) * 128] = acc
 
 
 def vmem(count):
@@ -511,24 +528,24 @@
     ram = pltpu.VMEM
     dma = lambda *s: pltpu.SemaphoreType.DMA(s)
     peers = NY * NC - 1
-    grad, feat, losses, rank = pl.pallas_call(
+    tokens, grad, row_loss = pl.pallas_call(
         main_kernel,
         out_shape=(
-            shape((4, LOCAL), F32), shape((PAD, D), BF16), shape((TOK, 8, 128), F32), shape((16, 128), F32),
+            shape((SEQ, D), BF16), shape((4, LOCAL), F32), shape((1, OUT), F32),
         ),
-        in_specs=[hbm] * 3 + vmem(1) + [hbm] * 2,
-        out_specs=tuple(vmem(4)),
+        in_specs=[hbm] * 3 + vmem(1) + [hbm] * 2 + vmem(1),
+        out_specs=tuple([hbm] + vmem(2)),
         scratch_shapes=[
             ram((SEQ, D), BF16), ram((SEQ, D), BF16), ram((1, SEQ), I32), ram((D, LOCAL), BF16), ram((1, LOCAL), F32),
-            dma(5), ram((1, 13 * 128), F32),
+            dma(5), dma(1), ram((16, 128), F32), ram((1, 13 * 128), F32),
             ram((PAD, D), BF16), ram((CAP, D), BF16), ram((CAP, D), BF16), ram((D, PAD), BF16),
         ]
         + [ram((CAP, w), F32) for w in WIDTHS] * 2
         + [ram((PAD, 128), F32)]
-        + [ram((CAP, 128), F32)] * 4
+        + [ram((PAD, 128), F32)] * 4
         + [
-            ram((8, PAD), F32), ram((peers, 8, PAD), F32), ram((PAD, 128), F32), ram((PAD, 128), F32),
-            ram((PAD, LANES), BF16), ram((PAD, LANES), BF16),
+            ram((2, 8, 512), F32), ram((peers, 2, 8, 512), F32),
+            ram((PAD, LOCAL), BF16),
             ram((CAP, D), F32), ram((D, LANES), F32), ram((CHUNKS, 64, LANES), F32),
             ram((CHUNKS, D, LANES), BF16),
             ram((CHUNKS, 2, 64, LANES // 2), BF16), ram((CHUNKS, 2, 64, LANES // 2), BF16),
@@ -538,7 +555,7 @@
             ram((NC, NY, 128, D), BF16), ram((NY, 128, D), BF16), ram((NY, 128, D), BF16),
             ram((NY - 1, 128, D), BF16), ram((NC, NY, 128, D), BF16),
             ram((4, 4, NX, 8, 128), F32),
-            dma(peers), dma(peers),
+            dma(peers, 2), dma(peers, 2),
             dma(3), dma(3),
             dma(6), dma(6),
             dma(CHUNKS, 6), dma(CHUNKS, 6),
@@ -546,19 +563,11 @@
             dma(8), dma(8),
         ],
         compiler_params=pltpu.CompilerParams(
-            collective_id=1, has_side_effects=True, vmem_limit_bytes=60 << 20
+            collective_id=1, has_side_effects=True, vmem_limit_bytes=62 << 20
         ),
         name="main",
-    )(student[0], teacher[0], mask, cot.reshape(1, 1), protos, center.reshape(1, LOCAL))
-
-    tokens, row_loss = pl.pallas_call(
-        place_kernel,
-        out_shape=(shape((SEQ, D), BF16), shape((1, OUT), F32)),
-        in_specs=vmem(4),
-        out_specs=tuple(vmem(2)),
-        compiler_params=pltpu.CompilerParams(vmem_limit_bytes=48 << 20),
-        name="place",
-    )(rank, feat, losses, perm.reshape(1, TOK))
+    )(student[0], teacher[0], mask, cot.reshape(1, 1), protos, center.reshape(1, LOCAL), perm.reshape(1, TOK))
+
     return tokens[None], grad, row_loss.reshape(OUT)
 
 

time: 89.1 us -> 87.9 us (0.987)
  Pallas kernels: 83.3 us -> 81.6 us
    pallas_call x2 -> x1, Pallas kernels: 83.3 us -> 81.6 us  [on_device(): pl.pallas_call(main_kernel, out_shape=(shape((SEQ, D), BF16), shape((4, L...]
    unnamed x9 -> x3, local copies, waits for them, and re-layouts: 4.16 us -> 4.81 us
where the time goes in v3:
time: 87.9 us; the launch traced here: 87.7 us
  Pallas kernels  81.6 us (93%)
  local copies, waits for them, and re-layouts  4.81 us (5%)
  between operations  1.29 us (1%)
    pallas_call x1, Pallas kernels, on_device(): pl.pallas_call(main_kernel, out_shape=(shape((SEQ, D), BF16), shape((4, L...  81.6 us
    unnamed x3, local copies, waits for them, and re-layouts  4.81 us

profile of v3, /device:TPU:2, one launch (start us, length us, event | category | flops | bytes accessed | tf_op | source)
XLA Modules:
  0.0 87.7 jit_solution(10967369216760344828)
XLA Ops:
  1.3 81.6 %main.1 = (bf16[1568,256]{1,0:T(8,128)(2,1)}, f32[4,4096]{1,0:T(4,128)}, f32[1,512]{1,0:T(1,128)}) custom-call(bf16[1568,256]{1,0:T(8,128)(2,1)} %bitcast.8, bf16[1568,256]{1,0:T(8,128)(2,1)} %bitcast.9, s32[1,1568]{1,0:T(1,128)} %mask_in.1, f32[1,1]{1,0:T(1,128)} %bitcast.7.cot, bf16[256,4096]{1,0:T(8,128)(2,1)} %protos_in.1, f32[1,4096]{1,0:T(1,128)} %bitcast.11, ...), custom_call_target="tpu_custom_call" | custom-call | tf_op jit(solution)/shard_map/main/pallas_call | solution.py:531
  82.8 2.1 %copy.14 = bf16[1,1568,256]{2,1,0:T(8,128)(2,1)} copy(bf16[1,1568,256]{2,1,0:T(8,128)(2,1)} %bitcast.10) | data formatting | bytes 1605632
  84.9 1.5 %copy.15 = f32[4,4096]{1,0:T(4,128)} copy(f32[4,4096]{1,0:T(4,128)} %get-tuple-element.13) | data formatting | bytes 131072
  86.4 1.3 %copy.16 = f32[512]{0:T(512)} copy(f32[512]{0:T(512)} %bitcast.12) | data formatting | bytes 4096

commit v4 on v3

--- a/solution.py
+++ b/solution.py
@@ -22,8 +22,8 @@
 TILE = 480
 TILES = CAP // TILE
 GROUP = 16
-STEP = 64
 ROWS = ((0, 512), (512, CAP - 512))
+STEPS = (256, 224)
 OUT = 512
 
 LOG2E = 1.4426950408889634
@@ -205,14 +205,14 @@
     peak_s[CAP:, :] = jnp.ones((PAD - CAP, 128), F32)
 
     def forward(r):
-        start, size = ROWS[r]
+        (start, size), step = ROWS[r], STEPS[r]
         for n in range(CHUNKS):
             scores(n, pl.ds(start, size))
             shift = lane_parts(center[:, columns(n)] * K_U)
 
             def gather(t, carry, n=n, shift=shift):
-                for k in range(STEP // GROUP):
-                    there = pl.ds(pl.multiple_of(start + t * STEP + k * GROUP, GROUP), GROUP)
+                for k in range(step // GROUP):
+                    there = pl.ds(pl.multiple_of(start + t * step + k * GROUP, GROUP), GROUP)
                     s = lane_parts(dots[n][there, :] * K_S)
                     u = [a * K_U - b for a, b in zip(lane_parts(targets[n][there, :]), shift)]
                     top_s = tree(jnp.maximum, s)
@@ -237,7 +237,7 @@
                     cross[there, :] = add_x
                 return carry
 
-            lax.fori_loop(0, size // STEP, gather, 0)
+            lax.fori_loop(0, size // step, gather, 0)
         at = slice(start, start + size)
         lane = lax.broadcasted_iota(I32, (size, 128), 1)
         top_s = jnp.max(peak_s[at, :], axis=1, keepdims=True)
@@ -292,12 +292,12 @@
         return (lse_s - all_x / all_u) * LN2
 
     def gradients(n, r):
-        start, size = ROWS[r]
+        (start, size), step = ROWS[r], STEPS[r]
         shift = lane_parts(center[:, columns(n)] * K_U)
 
         def tile(t, carry):
-            for k in range(STEP // GROUP):
-                there = pl.ds(pl.multiple_of(start + t * STEP + k * GROUP, GROUP), GROUP)
+            for k in range(step // GROUP):
+                there = pl.ds(pl.multiple_of(start + t * step + k * GROUP, GROUP), GROUP)
                 less_s, less_u = shift_s[there, :], shift_u[there, :]
                 s = lane_parts(dots[n][there, :])
                 u = lane_parts(targets[n][there, :])
@@ -307,7 +307,7 @@
                     grads[there, at : at + 128] = g.astype(BF16)
             return carry
 
-        lax.fori_loop(0, size // STEP, tile, 0)
+        lax.fori_loop(0, size // step, tile, 0)
 
     def gradient_rows(r):
         at = slice(ROWS[r][0], ROWS[r][0] + ROWS[r][1])
@@ -516,6 +516,22 @@
     for n in range(CHUNKS):
         for copy in relays[n] + directs[n] + sums[n] + nears[n] + ends[n]:
             copy.wait_send()
+
+
+def deliver_kernel(tokens, grad, row_loss, tokens_out, grad_out, loss_out, tokens_held, grad_held, loss_held, in_sem, out_sem):
+    stages = [(grad, grad_held, grad_out), (row_loss, loss_held, loss_out)]
+    for start in range(0, SEQ, 400):
+        part = pl.ds(start, min(400, SEQ - start))
+        stages.append((tokens.at[part], tokens_held.at[part], tokens_out.at[part]))
+    arrivals = [pltpu.make_async_copy(a, b, in_sem.at[i]) for i, (a, b, _) in enumerate(stages)]
+    leaves = [pltpu.make_async_copy(b, c, out_sem.at[i]) for i, (_, b, c) in enumerate(stages)]
+    for copy in arrivals:
+        copy.start()
+    for arrival, leave in zip(arrivals, leaves):
+        arrival.wait()
+        leave.start()
+    for copy in leaves:
+        copy.wait()
 
 
 def vmem(count):
@@ -568,6 +584,16 @@
         name="main",
     )(student[0], teacher[0], mask, cot.reshape(1, 1), protos, center.reshape(1, LOCAL), perm.reshape(1, TOK))
 
+    arrays = (tokens, grad, row_loss)
+    tokens, grad, row_loss = pl.pallas_call(
+        deliver_kernel,
+        out_shape=tuple(shape(a.shape, a.dtype) for a in arrays),
+        in_specs=[pl.BlockSpec(memory_space=pl.ANY)] * 3,
+        out_specs=tuple([pl.BlockSpec(memory_space=pltpu.HBM)] * 3),
+        scratch_shapes=[ram(a.shape, a.dtype) for a in arrays] + [dma(6), dma(6)],
+        compiler_params=pltpu.CompilerParams(vmem_limit_bytes=62 << 20),
+        name="deliver",
+    )(*arrays)
     return tokens[None], grad, row_loss.reshape(OUT)
 
 

time: 87.9 us -> 84.8 us (0.965)
  local copies, waits for them, and re-layouts: 4.81 us -> 0 us
  Pallas kernels: 81.6 us -> 83.2 us
    unnamed x3 -> x0, local copies, waits for them, and re-layouts: 4.81 us -> none
    pallas_call x0 -> x1, Pallas kernels: none -> 2.04 us  [on_device(): pl.pallas_call(deliver_kernel, out_shape=tuple((shape(a.shape, a.dtype) f...]
where the time goes in v4:
time: 84.8 us; the launch traced here: 84.7 us
  Pallas kernels  83.2 us (98%)
  between operations  1.45 us (2%)
    pallas_call x1, Pallas kernels, on_device(): pl.pallas_call(main_kernel, out_shape=(shape((SEQ, D), BF16), shape((4, L...  81.2 us
    pallas_call x1, Pallas kernels, on_device(): pl.pallas_call(deliver_kernel, out_shape=tuple((shape(a.shape, a.dtype) f...  2.04 us

profile of v4, /device:TPU:2, one launch (start us, length us, event | category | flops | bytes accessed | tf_op | source)
XLA Modules:
  0.0 84.7 jit_solution(14986883977959183529)
XLA Ops:
  1.3 81.2 %main.1 = (bf16[1568,256]{1,0:T(8,128)(2,1)}, f32[4,4096]{1,0:T(4,128)}, f32[1,512]{1,0:T(1,128)}) custom-call(bf16[1568,256]{1,0:T(8,128)(2,1)} %bitcast.8, bf16[1568,256]{1,0:T(8,128)(2,1)} %bitcast.9, s32[1,1568]{1,0:T(1,128)} %mask_in.1, f32[1,1]{1,0:T(1,128)} %bitcast.7.cot, bf16[256,4096]{1,0:T(8,128)(2,1)} %protos_in.1, f32[1,4096]{1,0:T(1,128)} %bitcast.10, ...), custom_call_target="tpu_custom_call" | custom-call | tf_op jit(solution)/shard_map/main/pallas_call | solution.py:547
  82.5 2.0 %deliver.1 = (bf16[1568,256]{1,0:T(8,128)(2,1)}, f32[4,4096]{1,0:T(4,128)}, f32[1,512]{1,0:T(1,128)}) custom-call(bf16[1568,256]{1,0:T(8,128)(2,1)} %get-tuple-element.9.tokens, f32[4,4096]{1,0:T(4,128)} %get-tuple-element.10.grad, f32[1,512]{1,0:T(1,128)} %get-tuple-element.11.row_loss), custom_call_target="tpu_custom_call" | custom-call | tf_op jit(solution)/shard_map/deliver/pallas_call | solution.py:588
